TPU v7x, 32 devices: a whole 2x2x4 slice. The times are simulated.
32 devices in a mesh: ctx: 16 (over z, y, x), fsdp: 2 (over core).
Axes of the slice: x: 2, y: 2, z: 4, core: 2. Of those that a mesh axis runs over, the one named last changes fastest.
Arguments:
- tokens: bfloat16 [4, 2048, 1024], P('fsdp', 'ctx'), may hold values from -6 to 6
- grad_out: bfloat16 [4, 2048, 1024], P('fsdp', 'ctx'), may hold values from -6 to 6
- ln1_gain: bfloat16 [1024], P('fsdp'), may hold values from 0.5 to 1.5
- ln1_bias: bfloat16 [1024], P('fsdp'), may hold values from -3 to 3
- w_qkv: bfloat16 [1024, 3072], P('fsdp'), may hold values from -0.1875 to 0.1875
- b_query: bfloat16 [1024], P('fsdp'), may hold values from -3 to 3
- b_value: bfloat16 [1024], P('fsdp'), may hold values from -0.29882812 to 0.29882812
- w_out: bfloat16 [1024, 1024], P('fsdp'), may hold values from -2 to 2
- b_out: bfloat16 [1024], P('fsdp'), may hold values from -3 to 3
- ln2_gain: bfloat16 [1024], P('fsdp'), may hold values from 0.5 to 1.5
- ln2_bias: bfloat16 [1024], P('fsdp'), may hold values from -3 to 3
- w_fc: bfloat16 [1024, 4096], P('fsdp'), may hold values from -0.1875 to 0.1875
- b_fc: bfloat16 [4096], P('fsdp'), may hold values from -3 to 3
- w_proj: bfloat16 [4096, 1024], P('fsdp'), may hold values from -0.09375 to 0.09375
- b_proj: bfloat16 [1024], P('fsdp'), may hold values from -3 to 3
Outputs:
- output: bfloat16 [4, 2048, 1024], P('fsdp', 'ctx')
- grad_tokens: bfloat16 [4, 2048, 1024], P('fsdp', 'ctx')
- grad_ln1_gain: float32 [1024], P('fsdp')
- grad_ln1_bias: float32 [1024], P('fsdp')
- grad_w_qkv: float32 [1024, 3072], P('fsdp')
- grad_b_query: float32 [1024], P('fsdp')
- grad_b_value: float32 [1024], P('fsdp')
- grad_w_out: float32 [1024, 1024], P('fsdp')
- grad_b_out: float32 [1024], P('fsdp')
- grad_ln2_gain: float32 [1024], P('fsdp')
- grad_ln2_bias: float32 [1024], P('fsdp')
- grad_w_fc: float32 [1024, 4096], P('fsdp')
- grad_b_fc: float32 [4096], P('fsdp')
- grad_w_proj: float32 [4096, 1024], P('fsdp')
- grad_b_proj: float32 [1024], P('fsdp')
All inputs are finite; a program needn't handle non-finite values.
Results may differ from a plain program's by a relative error of at most 0.017.
Values may be sent and summed in bfloat16 or wider, within the bound.
A program may use at most 384 MiB of HBM per device.

v0:
```python
from functools import partial
import math

import jax
import jax.numpy as jnp
from jax import lax
from jax.sharding import PartitionSpec as P

HEADS = 16


def norm(inputs, gain, shift):
    mean = jnp.mean(inputs, axis=-1, keepdims=True)
    centred = inputs - mean
    spread = jnp.mean(centred * centred, axis=-1, keepdims=True)
    return centred * lax.rsqrt(spread + 1e-05) * gain + shift


def split_heads(values, heads):
    return values.reshape(values.shape[0], values.shape[1], heads, values.shape[2] // heads)


def inner(left, right):
    return lax.dot_general(
        left, right, (((0,), (0,)), ((), ())), preferred_element_type=jnp.float32
    )


def times_transposed(left, right):
    return lax.dot_general(
        left, right, (((1,), (1,)), ((), ())), preferred_element_type=jnp.float32
    )


def local(
    tokens,
    grad_out,
    ln1_gain,
    ln1_bias,
    w_qkv,
    b_query,
    b_value,
    w_out,
    b_out,
    ln2_gain,
    ln2_bias,
    w_fc,
    b_fc,
    w_proj,
    b_proj,
):
    gathered = (
        lax.all_gather(ln1_gain, "fsdp", axis=0, tiled=True),
        lax.all_gather(ln1_bias, "fsdp", axis=0, tiled=True),
        lax.all_gather(w_qkv, "fsdp", axis=0, tiled=True),
        lax.all_gather(b_query, "fsdp", axis=0, tiled=True),
        lax.all_gather(b_value, "fsdp", axis=0, tiled=True),
        lax.all_gather(w_out, "fsdp", axis=0, tiled=True),
        lax.all_gather(b_out, "fsdp", axis=0, tiled=True),
        lax.all_gather(ln2_gain, "fsdp", axis=0, tiled=True),
        lax.all_gather(ln2_bias, "fsdp", axis=0, tiled=True),
        lax.all_gather(w_fc, "fsdp", axis=0, tiled=True),
        lax.all_gather(b_fc, "fsdp", axis=0, tiled=True),
        lax.all_gather(w_proj, "fsdp", axis=0, tiled=True),
        lax.all_gather(b_proj, "fsdp", axis=0, tiled=True),
    )
    (
        gain_one,
        shift_one,
        wide_qkv,
        bias_query,
        bias_value,
        wide_out,
        bias_out,
        gain_two,
        shift_two,
        wide_fc,
        bias_fc,
        wide_proj,
        bias_proj,
    ) = gathered
    gain_one = gain_one.astype(jnp.float32)
    shift_one = shift_one.astype(jnp.float32)
    gain_two = gain_two.astype(jnp.float32)
    shift_two = shift_two.astype(jnp.float32)
    seqs, block, width = tokens.shape
    rows = seqs * block
    heads = HEADS
    head_size = width // heads
    scale = 1.0 / math.sqrt(head_size)
    own_pos = lax.axis_index("ctx") * block + jnp.arange(block, dtype=jnp.int32)
    inputs = tokens.astype(jnp.float32).reshape(rows, width)
    low_one = norm(inputs, gain_one, shift_one).astype(jnp.bfloat16)
    packed = jnp.dot(low_one, wide_qkv, preferred_element_type=jnp.float32)
    query = (
        (packed[:, :width] + bias_query.astype(jnp.float32))
        .astype(jnp.bfloat16)
        .reshape(seqs, block, width)
    )
    keys = packed[:, width : 2 * width].astype(jnp.bfloat16).reshape(seqs, block, width)
    values = (
        (packed[:, 2 * width :] + bias_value.astype(jnp.float32))
        .astype(jnp.bfloat16)
        .reshape(seqs, block, width)
    )
    query_heads = split_heads(query, heads)
    key_heads = split_heads(keys, heads)
    value_heads = split_heads(values, heads)
    top = jnp.full((seqs, heads, block), -1e30, jnp.float32)
    key_piece = lax.all_gather(keys, "ctx", axis=1, tiled=True)
    value_piece = lax.all_gather(values, "ctx", axis=1, tiled=True)
    count = key_piece.shape[1]
    scores = (
        jnp.einsum(
            "sbhe,sphe->shbp",
            query_heads,
            split_heads(key_piece, heads),
            preferred_element_type=jnp.float32,
        )
        * scale
    )
    allowed = jnp.arange(count, dtype=jnp.int32)[None, :] <= own_pos[:, None]
    masked = jnp.where(allowed, scores, -1e30)
    new_top = jnp.maximum(top, jnp.max(masked, axis=-1))
    weights = jnp.where(allowed, jnp.exp(masked - new_top[..., None]), 0.0)
    total = jnp.sum(weights, axis=-1)
    summed = jnp.einsum(
        "shbp,sphe->shbe",
        weights.astype(jnp.bfloat16),
        split_heads(value_piece, heads),
        preferred_element_type=jnp.float32,
    )
    top, total, summed = (new_top, total, summed)
    attended = summed / total[..., None]
    row_lse = top + jnp.log(total)
    low_att = attended.transpose(0, 2, 1, 3).reshape(rows, width).astype(jnp.bfloat16)
    mixed = (
        inputs
        + jnp.dot(low_att, wide_out, preferred_element_type=jnp.float32)
        + bias_out.astype(jnp.float32)
    )
    low_two = norm(mixed, gain_two, shift_two).astype(jnp.bfloat16)
    hidden = jnp.dot(low_two, wide_fc, preferred_element_type=jnp.float32) + bias_fc.astype(
        jnp.float32
    )
    low_act = jax.nn.gelu(hidden, approximate=True).astype(jnp.bfloat16)
    result = (
        mixed
        + jnp.dot(low_act, wide_proj, preferred_element_type=jnp.float32)
        + bias_proj.astype(jnp.float32)
    )
    output = result.astype(jnp.bfloat16).reshape(seqs, block, width)
    regathered = (
        lax.all_gather(ln1_gain, "fsdp", axis=0, tiled=True),
        lax.all_gather(ln1_bias, "fsdp", axis=0, tiled=True),
        lax.all_gather(w_qkv, "fsdp", axis=0, tiled=True),
        lax.all_gather(b_query, "fsdp", axis=0, tiled=True),
        lax.all_gather(b_value, "fsdp", axis=0, tiled=True),
        lax.all_gather(w_out, "fsdp", axis=0, tiled=True),
        lax.all_gather(b_out, "fsdp", axis=0, tiled=True),
        lax.all_gather(ln2_gain, "fsdp", axis=0, tiled=True),
        lax.all_gather(ln2_bias, "fsdp", axis=0, tiled=True),
        lax.all_gather(w_fc, "fsdp", axis=0, tiled=True),
        lax.all_gather(b_fc, "fsdp", axis=0, tiled=True),
        lax.all_gather(w_proj, "fsdp", axis=0, tiled=True),
        lax.all_gather(b_proj, "fsdp", axis=0, tiled=True),
    )
    back_qkv = regathered[2]
    back_out = regathered[5]
    back_fc = regathered[9]
    back_proj = regathered[11]
    grad_rows = grad_out.reshape(rows, width)
    grad_float = grad_rows.astype(jnp.float32)
    grad_b_proj = jnp.sum(grad_float, axis=0)
    grad_w_proj = inner(low_act, grad_rows)
    grad_act = times_transposed(grad_rows, back_proj)
    _, gelu_back = jax.vjp(partial(jax.nn.gelu, approximate=True), hidden)
    low_hidden = gelu_back(grad_act)[0].astype(jnp.bfloat16)
    grad_b_fc = jnp.sum(low_hidden.astype(jnp.float32), axis=0)
    grad_w_fc = inner(low_two, low_hidden)
    grad_normed_two = times_transposed(low_hidden, back_fc)
    _, norm_two_back = jax.vjp(norm, mixed, gain_two, shift_two)
    grad_mixed_part, grad_ln2_gain, grad_ln2_bias = norm_two_back(grad_normed_two)
    grad_mixed = grad_float + grad_mixed_part
    low_branch = grad_mixed.astype(jnp.bfloat16)
    grad_b_out = jnp.sum(low_branch.astype(jnp.float32), axis=0)
    grad_w_out = inner(low_att, low_branch)
    low_grad_att = (
        times_transposed(low_branch, back_out).astype(jnp.bfloat16).reshape(seqs, block, width)
    )
    grad_att_heads = split_heads(low_grad_att, heads)
    row_delta = jnp.einsum("sbhe,shbe->shb", grad_att_heads.astype(jnp.float32), attended)
    key_piece = lax.all_gather(keys, "ctx", axis=1, tiled=True)
    value_piece = lax.all_gather(values, "ctx", axis=1, tiled=True)
    count = key_piece.shape[1]
    key_part = split_heads(key_piece, heads)
    scores = (
        jnp.einsum("sbhe,sphe->shbp", query_heads, key_part, preferred_element_type=jnp.float32)
        * scale
    )
    allowed = jnp.arange(count, dtype=jnp.int32)[None, :] <= own_pos[:, None]
    probs = jnp.where(allowed, jnp.exp(jnp.where(allowed, scores, -1e30) - row_lse[..., None]), 0.0)
    dprobs = jnp.einsum(
        "sbhe,sphe->shbp",
        grad_att_heads,
        split_heads(value_piece, heads),
        preferred_element_type=jnp.float32,
    )
    grad_scores = (probs * (dprobs - row_delta[..., None])).astype(jnp.bfloat16)
    grad_query_heads = (
        jnp.einsum("shbp,sphe->shbe", grad_scores, key_part, preferred_element_type=jnp.float32)
        * scale
    )
    lse_all, delta_all = (
        lax.all_gather(row_lse.transpose(0, 2, 1), "ctx", axis=1, tiled=True),
        lax.all_gather(row_delta.transpose(0, 2, 1), "ctx", axis=1, tiled=True),
    )
    query_piece = lax.all_gather(query, "ctx", axis=1, tiled=True)
    grad_piece = lax.all_gather(low_grad_att, "ctx", axis=1, tiled=True)
    count = query_piece.shape[1]
    query_part = split_heads(query_piece, heads)
    grad_part = split_heads(grad_piece, heads)
    lse_part = lse_all.transpose(0, 2, 1)
    delta_part = delta_all.transpose(0, 2, 1)
    scores = (
        jnp.einsum("sphe,sbhe->shpb", query_part, key_heads, preferred_element_type=jnp.float32)
        * scale
    )
    allowed = own_pos[None, :] <= jnp.arange(count, dtype=jnp.int32)[:, None]
    probs = jnp.where(
        allowed, jnp.exp(jnp.where(allowed, scores, -1e30) - lse_part[..., None]), 0.0
    )
    grad_values = jnp.einsum(
        "shpb,sphe->sbhe", probs.astype(jnp.bfloat16), grad_part, preferred_element_type=jnp.float32
    )
    dprobs = jnp.einsum(
        "sphe,sbhe->shpb", grad_part, value_heads, preferred_element_type=jnp.float32
    )
    grad_scores = (probs * (dprobs - delta_part[..., None])).astype(jnp.bfloat16)
    grad_keys = (
        jnp.einsum("shpb,sphe->sbhe", grad_scores, query_part, preferred_element_type=jnp.float32)
        * scale
    )
    low_grad_query = (
        grad_query_heads.transpose(0, 2, 1, 3).reshape(rows, width).astype(jnp.bfloat16)
    )
    low_grad_keys = grad_keys.reshape(rows, width).astype(jnp.bfloat16)
    low_grad_values = grad_values.reshape(rows, width).astype(jnp.bfloat16)
    grad_b_query = jnp.sum(low_grad_query.astype(jnp.float32), axis=0)
    grad_b_value = jnp.sum(low_grad_values.astype(jnp.float32), axis=0)
    grad_packed = jnp.concatenate([low_grad_query, low_grad_keys, low_grad_values], axis=1)
    grad_w_qkv = inner(low_one, grad_packed)
    grad_normed_one = times_transposed(grad_packed, back_qkv)
    _, norm_one_back = jax.vjp(norm, inputs, gain_one, shift_one)
    grad_input_part, grad_ln1_gain, grad_ln1_bias = norm_one_back(grad_normed_one)
    grad_tokens = (grad_mixed + grad_input_part).astype(jnp.bfloat16).reshape(seqs, block, width)
    shard_parts = (
        lax.psum_scatter(grad_ln1_gain, "fsdp", scatter_dimension=0, tiled=True),
        lax.psum_scatter(grad_ln1_bias, "fsdp", scatter_dimension=0, tiled=True),
        lax.psum_scatter(grad_w_qkv, "fsdp", scatter_dimension=0, tiled=True),
        lax.psum_scatter(grad_b_query, "fsdp", scatter_dimension=0, tiled=True),
        lax.psum_scatter(grad_b_value, "fsdp", scatter_dimension=0, tiled=True),
        lax.psum_scatter(grad_w_out, "fsdp", scatter_dimension=0, tiled=True),
        lax.psum_scatter(grad_b_out, "fsdp", scatter_dimension=0, tiled=True),
        lax.psum_scatter(grad_ln2_gain, "fsdp", scatter_dimension=0, tiled=True),
        lax.psum_scatter(grad_ln2_bias, "fsdp", scatter_dimension=0, tiled=True),
        lax.psum_scatter(grad_w_fc, "fsdp", scatter_dimension=0, tiled=True),
        lax.psum_scatter(grad_b_fc, "fsdp", scatter_dimension=0, tiled=True),
        lax.psum_scatter(grad_w_proj, "fsdp", scatter_dimension=0, tiled=True),
        lax.psum_scatter(grad_b_proj, "fsdp", scatter_dimension=0, tiled=True),
    )
    (
        part_gain_one,
        part_shift_one,
        part_qkv,
        part_query,
        part_value,
        part_out,
        part_bias_out,
        part_gain_two,
        part_shift_two,
        part_fc,
        part_bias_fc,
        part_proj,
        part_bias_proj,
    ) = shard_parts
    totals = lax.psum(
        (
            part_gain_one,
            part_shift_one,
            part_qkv,
            part_query,
            part_value,
            part_out,
            part_bias_out,
            part_gain_two,
            part_shift_two,
            part_fc,
            part_bias_fc,
            part_proj,
            part_bias_proj,
        ),
        "ctx",
    )
    return (
        output,
        grad_tokens,
        totals[0],
        totals[1],
        totals[2],
        totals[3],
        totals[4],
        totals[5],
        totals[6],
        totals[7],
        totals[8],
        totals[9],
        totals[10],
        totals[11],
        totals[12],
    )


def solution(mesh):
    in_specs = (
        P("fsdp", "ctx", None),
        P("fsdp", "ctx", None),
        P("fsdp"),
        P("fsdp"),
        P("fsdp", None),
        P("fsdp"),
        P("fsdp"),
        P("fsdp", None),
        P("fsdp"),
        P("fsdp"),
        P("fsdp"),
        P("fsdp", None),
        P("fsdp"),
        P("fsdp", None),
        P("fsdp"),
    )
    out_specs = (
        P("fsdp", "ctx", None),
        P("fsdp", "ctx", None),
        P("fsdp"),
        P("fsdp"),
        P("fsdp", None),
        P("fsdp"),
        P("fsdp"),
        P("fsdp", None),
        P("fsdp"),
        P("fsdp"),
        P("fsdp"),
        P("fsdp", None),
        P("fsdp"),
        P("fsdp", None),
        P("fsdp"),
    )
    return jax.shard_map(local, mesh=mesh, in_specs=in_specs, out_specs=out_specs, check_vma=False)
```

profile of v0, /device:TPU:0, one launch (start us, length us, event | category | flops | bytes accessed | tf_op | source)
XLA Modules:
  0.0 1353.1 jit_solution(8419389541935888166)
XLA Ops:
  8.0 0.7 all-gather.27.cloned.1.call-update
  8.7 0.7 reshape.201
  9.4 1.9 all-gather.1
  12.0 1.8 all-gather
  13.8 1.2 convert_reduce_fusion.5
  15.0 1.3 multiply_reduce_fusion.6
  17.2 11.8 all-gather.17.cloned.1.call-done
  29.1 4.6 fusion.77
  33.7 1.7 copy-done.13
  35.3 0.9 slice.23
  36.3 1.8 all-gather.2
  38.1 1.8 all-gather.3
  39.9 3.2 fusion.37
  44.3 0.7 all-gather.29.cloned.1.call-update
  45.1 1.8 all-gather.4
  46.9 1.8 all_gather.75
  48.7 1.8 all-gather.6
  50.5 2.1 all-gather.5
  52.8 1.8 reshape.226
  54.6 7.8 fusion.78
  62.4 106.6 %all-gather.19.cloned.1.call-done = bf16[2,2048,1024]{2,1,0:T(8,128)(2,1)} async-done(((bf16[2,128,1024]{2,1,0:T(8,128)(2,1)}), bf16[2,2048,1024]{2,1,0:T(8,128)(2,1)}) %all-gather.19.cloned.1.call-update) | async-done | bytes 8388624 | tf_op jit(solution)/shard_map/all_gather | solution.py:110
  168.9 11.7 copy.51
  180.7 101.8 %all-gather.21.cloned.1.call-done = bf16[2,2048,1024]{2,1,0:T(8,128)(2,1)} async-done(((bf16[2,128,1024]{2,1,0:T(8,128)(2,1)}), bf16[2,2048,1024]{2,1,0:T(8,128)(2,1)}) %all-gather.21.cloned.1.call-update) | async-done | bytes 8388624 | tf_op jit(solution)/shard_map/all_gather | solution.py:111
  282.5 11.9 copy.53
  294.4 20.2 %fusion.3 = (f32[2,16,128]{2,1,0:T(8,128)S(1)}, f32[2,16,128,2048]{3,2,1,0:T(8,128)}) fusion(pred[128,2048]{1,0:T(8,128)(4,1)S(1)} %iota_compare_fusion.1, bf16[2,2048,16,64]{1,3,2,0:T(8,128)(2,1)} %bitcast.129, bf16[2,128,16,64]{3,2,1,0:T(8,128)(2,1)S(1)} %reshape.226), kind=kOutput, calls=%fused_computation.8 | convolution fusion | flops 1098903552 | bytes 42745856 | tf_op jit(solution)/shard_map/sbhe,sphe->shbp/dot_general | solution.py:114
  314.7 16.1 %fusion = f32[2,16,128]{2,1,0:T(8,128)S(1)} fusion(f32[2,16,128,2048]{3,2,1,0:T(8,128)} %get-tuple-element.55, f32[2,16,128]{2,1,0:T(8,128)S(1)} %broadcast_maximum_fusion, pred[128,2048]{1,0:T(8,128)(4,1)S(1)} %iota_compare_fusion.1), kind=kLoop, calls=%fused_computation.5 | loop fusion | flops 41938944 | bytes 33849344 | tf_op jit(solution)/shard_map/reduce_sum | solution.py:126
  330.8 15.3 %fusion.42 = (bf16[2,128,16,64]{1,3,2,0:T(8,128)(2,1)S(1)}, f32[2,16,128,64]{2,3,1,0:T(8,128)}) fusion(f32[2,128,16]{1,2,0:T(8,128)S(1)} %bitcast.154, bf16[2,2048,16,64]{1,3,2,0:T(8,128)(2,1)S(1)} %bitcast.137, f32[2,16,128,2048]{3,2,1,0:T(8,128)} %get-tuple-element.55, f32[2,16,128]{2,1,0:T(8,128)S(1)} %broadcast_maximum_fusion, ...), kind=kOutput, calls=%fused_computation.54 | convolution fusion | flops 1116209152 | bytes 43810816 | tf_op jit(solution)/shard_map/shbp,sphe->shbe/dot_general | solution.py:127
  346.6 2.4 fusion.74
  349.4 12.8 convert_reduce_fusion
  362.2 3.2 multiply_reduce_fusion.1
  365.8 1.0 copy-done.4
  366.7 0.8 convert_reduce_fusion.2
  367.6 1.5 convolution_convert_fusion
  369.2 2.7 fusion.46
  371.9 10.6 fusion.68
  382.7 10.7 fusion.69
  393.7 0.8 copy-done.10
  395.2 1.6 reshape.228
  397.6 1.5 multiply_reduce_fusion
  399.1 22.5 %convert_reduce_fusion.4 = (f32[16,64]{1,0:T(8,128)S(1)}, bf16[2,16,128,64]{2,3,1,0:T(8,128)(2,1)S(1)}) fusion(bf16[2,2048,16,64]{1,3,2,0:T(8,128)(2,1)} %bitcast.130, f32[2,16,128,2048]{3,2,1,0:T(8,128)} %get-tuple-element.55, f32[2,16,128]{2,1,0:T(8,128)S(1)} %multiply_reduce_fusion, f32[2,16,128]{2,1,0:T(8,128)S(1)} %log_add_fusion, ...), kind=kOutput, calls=%fused_computation.63 | convolution fusion | flops 2207251456 | bytes 51679232 | tf_op jit(solution)/shard_map/shbp,sphe->shbe/dot_general | solution.py:211
  422.1 10.6 all-gather.29.cloned.1.call-done
  432.7 11.7 copy.58
  444.4 43.0 %all_gather.81 = f32[2,2048,16]{1,2,0:T(8,128)} all-gather(f32[2,128,16]{1,2,0:T(8,128)S(1)} %bitcast.164), channel_id=1, replica_groups=mesh['ctx'=16,'fsdp'=2] {'ctx'}, dimensions={1}, use_global_device_ids=true | all-gather | bytes 278528 | tf_op jit(solution)/shard_map/all_gather | solution.py:216
  487.3 42.0 %all_gather.79 = f32[2,2048,16]{1,2,0:T(8,128)} all-gather(f32[2,128,16]{1,2,0:T(8,128)S(1)} %bitcast_add_fusion), channel_id=1, replica_groups=mesh['ctx'=16,'fsdp'=2] {'ctx'}, dimensions={1}, use_global_device_ids=true | all-gather | bytes 278528 | tf_op jit(solution)/shard_map/all_gather | solution.py:215
  529.4 15.7 %fusion.40 = f32[2,16,2048,128]{3,2,1,0:T(8,128)} fusion(bf16[2,2048,16,64]{1,3,2,0:T(8,128)(2,1)} %bitcast.127, bf16[2,128,16,64]{3,2,1,0:T(8,128)(2,1)S(1)} %reshape.227), kind=kOutput, calls=%fused_computation.51 | convolution fusion | flops 1073741824 | bytes 42467328 | tf_op jit(solution)/shard_map/sphe,sbhe->shpb/dot_general | solution.py:226
  545.2 6.2 all-gather.31.cloned.1.call-done
  551.4 12.1 copy.61
  563.5 28.4 %multiply_convert_fusion.19 = bf16[2,16,2048,128]{3,2,1,0:T(8,128)(2,1)} fusion(f32[2,16,2048,128]{3,2,1,0:T(8,128)} %fusion.40, f32[2,16,2048]{2,1,0:T(8,128)S(1)} %bitcast.157, f32[2,16,2048]{2,1,0:T(8,128)S(1)} %bitcast.155, pred[2048,128]{1,0:T(8,128)(4,1)S(1)} %iota_compare_fusion, ...), kind=kOutput, calls=%fused_computation.clone.clone.clone.clone.clone.clone.clone.clone.1 | convolution fusion | flops 1132462080 | bytes 60030976 | tf_op jit(solution)/shard_map/sphe,sbhe->shpb/dot_general | solution.py:236
  591.9 12.0 fusion.35
  604.4 21.0 %convert_reduce_fusion.3 = (f32[16,64]{1,0:T(8,128)S(1)}, bf16[2,16,64,128]{3,2,1,0:T(8,128)(2,1)S(1)}) fusion(bf16[2,2048,16,64]{1,3,2,0:T(8,128)(2,1)S(1)} %bitcast.139, f32[2,16,2048,128]{3,2,1,0:T(8,128)} %fusion.40, f32[2,16,2048]{2,1,0:T(8,128)S(1)} %bitcast.156, pred[2048,128]{1,0:T(8,128)(4,1)S(1)} %iota_compare_fusion), kind=kOutput, calls=%fused_computation.62 | convolution fusion | flops 1116470272 | bytes 42995712 | tf_op jit(solution)/shard_map/shpb,sphe->sbhe/dot_general | solution.py:233
  626.2 6.4 fusion.79
  633.0 21.5 %reduce-scatter.5.cloned.1.call-done = f32[512,3072]{1,0:T(8,128)} async-done(((f32[1024,3072]{1,0:T(8,128)}), f32[512,3072]{1,0:T(8,128)}) %reduce-scatter.5.cloned.1.call-update) | async-done | bytes 6291472 | tf_op jit(solution)/shard_map/reduce_scatter | solution.py:260
  655.2 1.8 all-gather.7
  659.0 8.2 fusion.29
  667.4 6.6 fusion.70
  674.6 3.6 all-reduce.11
  678.8 81.7 %all-reduce.9 = (f32[512]{0:T(512)}, f32[512]{0:T(512)}, f32[512]{0:T(512)}, f32[512]{0:T(512)}, f32[512]{0:T(512)}, /*index=5*/f32[512]{0:T(512)}, f32[512]{0:T(512)}, f32[2048]{0:T(1024)}, f32[512]{0:T(512)}) all-reduce(f32[512]{0:T(512)S(1)} %dynamic-slice.1, ...), channel_id=1, replica_groups=mesh['ctx'=16,'fsdp'=2] {'ctx'}, use_global_device_ids=true, to_apply=%region_12.13 | all-reduce | flops 6144 | bytes 49152 | tf_op jit(solution)/shard_map/psum | solution.py:287
  760.6 1.3 add_convert_fusion
  761.8 566.7 %all-reduce.14.cloned.1.call-done = (f32[512,3072]{1,0:T(8,128)}, f32[512,1024]{1,0:T(8,128)}, f32[512,4096]{1,0:T(8,128)}, f32[2048,1024]{1,0:T(8,128)}) async-done(((f32[512,3072]{1,0:T(8,128)}, f32[512,1024]{1,0:T(8,128)}, f32[512,4096]{1,0:T(8,128)}, f32[2048,1024]{1,0:T(8,128)}), (f32[512,3072]{1,0:T(8,128)}, f32[512,1024]{1,0:T(8,128)}, f32[512,4096]{1,0:T(8,128)}, ...) | async-done | bytes 25165840 | tf_op jit(solution)/shard_map/psum | solution.py:287
  1328.5 6.9 copy.118
  1335.4 1.3 copy.119
  1337.2 4.3 copy.120
  1341.5 1.5 slice-done.1
  1343.0 3.4 copy.121
  (186 shorter events, 12.6 us)
Async XLA Ops:
  7.2 9.7 copy-start
  7.2 21.9 %all-gather.17.cloned.1.call-start = ((), (), s32[]{:S(2)}) async-start(), calls=%async_computation.4 | async-start | bytes 9437184 | tf_op jit(solution)/shard_map/all_gather | solution.py:55
  7.9 46.7 %all-gather.27.cloned.1.call-start = ((), (), s32[]{:S(2)}) async-start(), calls=%async_computation.9 | async-start | bytes 12582912 | tf_op jit(solution)/shard_map/all_gather | solution.py:64
  8.7 160.3 %all-gather.19.cloned.1.call-start = ((), (), s32[]{:S(2)}) async-start(), calls=%async_computation.5 | async-start | bytes 8912896 | tf_op jit(solution)/shard_map/all_gather | solution.py:110
  13.8 3.1 copy-start.23
  15.0 1.9 copy-start.27
  16.3 0.6 copy-start.31
  16.4 0.6 copy-start.29
  17.2 25.9 %copy-start.15 = (bf16[256,1024]{1,0:T(8,128)(2,1)}, bf16[256,1024]{1,0:T(8,128)(2,1)S(1)}, u32[]{:S(2)}) copy-start(bf16[256,1024]{1,0:T(8,128)(2,1)S(1)} %add_convert_fusion.2) | copy-start | bytes 1572868
  17.2 19.1 %copy-start.38 = (bf16[512]{0:T(512)(128)(2,1)S(1)}, bf16[512]{0:T(512)(128)(2,1)}, u32[]{:S(2)}) copy-start(bf16[512]{0:T(512)(128)(2,1)} %param.20) | copy-start | bytes 3076
  17.2 20.9 %copy-start.39 = (bf16[512]{0:T(512)(128)(2,1)S(1)}, bf16[512]{0:T(512)(128)(2,1)}, u32[]{:S(2)}) copy-start(bf16[512]{0:T(512)(128)(2,1)} %param.21) | copy-start | bytes 3076
  33.6 1.7 copy-start.13
  35.3 9.7 copy-start.40
  35.3 11.6 copy-start.35
  35.3 13.4 copy-start.41
  35.3 15.2 %copy-start.42 = (bf16[512]{0:T(512)(128)(2,1)S(1)}, bf16[512]{0:T(512)(128)(2,1)}, u32[]{:S(2)}) copy-start(bf16[512]{0:T(512)(128)(2,1)} %param.24) | copy-start | bytes 3076
  35.3 19.3 %copy-start.8 = (bf16[2,128,1024]{2,1,0:T(8,128)(2,1)S(1)}, bf16[2,128,1024]{2,1,0:T(8,128)(2,1)}, u32[]{:S(2)}) copy-start(bf16[2,128,1024]{2,1,0:T(8,128)(2,1)} %param.16) | copy-start | bytes 1572868
  36.2 246.3 %all-gather.21.cloned.1.call-start = ((), (), s32[]{:S(2)}) async-start(), calls=%async_computation.6 | async-start | bytes 8912896 | tf_op jit(solution)/shard_map/all_gather | solution.py:111
  43.1 303.5 %all-gather.23.cloned.1.call-start = ((), (), s32[]{:S(2)}) async-start(), calls=%async_computation.7 | async-start | bytes 3145728 | tf_op jit(solution)/shard_map/all_gather | solution.py:58
  43.7 305.7 %all-gather.25.cloned.1.call-start = ((), (), s32[]{:S(2)}) async-start(), calls=%async_computation.8 | async-start | bytes 12582912 | tf_op jit(solution)/shard_map/all_gather | solution.py:62
  44.3 388.4 %all-gather.29.cloned.1.call-start = ((), (), s32[]{:S(2)}) async-start(), calls=%async_computation.10 | async-start | bytes 8912896 | tf_op jit(solution)/shard_map/all_gather | solution.py:218
  45.0 506.4 %all-gather.31.cloned.1.call-start = ((), (), s32[]{:S(2)}) async-start(), calls=%async_computation.11 | async-start | bytes 8912896 | tf_op jit(solution)/shard_map/all_gather | solution.py:219
  314.7 16.1 %copy-start.6 = (bf16[2,2048,1024]{1,2,0:T(8,128)(2,1)S(1)}, bf16[2,2048,1024]{1,2,0:T(8,128)(2,1)}, u32[]{:S(2)}) copy-start(bf16[2,2048,1024]{1,2,0:T(8,128)(2,1)} %copy.53) | copy-start | bytes 25165828
  349.0 22.9 %copy-start.2 = (f32[256,1024]{1,0:T(8,128)}, f32[256,1024]{1,0:T(8,128)S(1)}, u32[]{:S(2)}) copy-start(f32[256,1024]{1,0:T(8,128)S(1)} %get-tuple-element.59) | copy-start | bytes 3145732
  349.4 12.8 copy-start.44
  362.2 3.6 copy-start.19
  362.2 5.4 copy-start.14
  365.7 1.0 copy-start.4
  365.8 16.7 %copy-start.33 = (f32[256]{0:T(256)}, f32[256]{0:T(256)S(1)}, u32[]{:S(2)}) copy-start(f32[256]{0:T(256)S(1)} %negate_multiply_fusion.1) | copy-start | bytes 3076
  369.1 263.8 %reduce-scatter.7.cloned.1.call-start = ((), (), s32[]{:S(2)}) async-start(), calls=%async_computation.13 | async-start | bytes 6291456 | tf_op jit(solution)/shard_map/reduce_scatter | solution.py:263
  371.9 261.1 %reduce-scatter.9.cloned.1.call-start = ((), (), s32[]{:S(2)}) async-start(), calls=%async_computation.14 | async-start | bytes 25165824 | tf_op jit(solution)/shard_map/reduce_scatter | solution.py:267
  382.5 250.4 %reduce-scatter.11.cloned.1.call-start = ((), (), s32[]{:S(2)}) async-start(), calls=%async_computation.15 | async-start | bytes 25165824 | tf_op jit(solution)/shard_map/reduce_scatter | solution.py:269
  393.5 1.0 copy-start.10
  393.5 1.7 copy-start.11
  393.5 3.3 copy-start.18
  393.5 261.0 %reduce-scatter.5.cloned.1.call-start = ((), (), s32[]{:S(2)}) async-start(), calls=%async_computation.12 | async-start | bytes 18874368 | tf_op jit(solution)/shard_map/reduce_scatter | solution.py:260
  545.2 18.3 %copy-start.20 = (bf16[2,128,16,64]{3,2,1,0:T(8,128)(2,1)S(1)}, bf16[2,128,16,64]{3,2,1,0:T(8,128)(2,1)}, u32[]{:S(2)}) copy-start(bf16[2,128,16,64]{3,2,1,0:T(8,128)(2,1)} %reshape.228) | copy-start | bytes 1572868
  545.2 18.3 %copy-start.21 = (f32[2,2048,16]{1,2,0:T(8,128)S(1)}, f32[2,2048,16]{1,2,0:T(8,128)}, u32[]{:S(2)}) copy-start(f32[2,2048,16]{1,2,0:T(8,128)} %all_gather.79) | copy-start | bytes 786436
  545.2 18.3 %copy-start.22 = (f32[2,2048,16]{1,2,0:T(8,128)S(1)}, f32[2,2048,16]{1,2,0:T(8,128)}, u32[]{:S(2)}) copy-start(f32[2,2048,16]{1,2,0:T(8,128)} %all_gather.81) | copy-start | bytes 786436
  591.9 12.5 copy-start.7
  604.4 21.7 %copy-start.16 = (bf16[256,1024]{1,0:T(8,128)(2,1)S(1)}, bf16[256,1024]{1,0:T(8,128)(2,1)}, u32[]{:S(2)}) copy-start(bf16[256,1024]{1,0:T(8,128)(2,1)} %copy-done.15) | copy-start | bytes 1572868
  626.2 6.4 copy-start.12
  632.6 695.9 %all-reduce.14.cloned.1.call-start = ((), (), s32[]{:S(2)}) async-start(), calls=%async_computation.16 | async-start | bytes 50331648 | tf_op jit(solution)/shard_map/psum | solution.py:287
  654.5 0.7 copy-start.43
  654.5 2.5 copy-start.45
  654.5 4.4 copy-start.9
  654.5 4.5 copy-start.3
  659.0 8.4 copy-start.1
  659.0 8.4 copy-start.24
  659.0 8.4 copy-start.28
  667.3 6.8 copy-start.32
  667.3 6.8 copy-start.30
  667.3 7.3 copy-start.25
  667.3 7.3 copy-start.26
  667.3 7.3 copy-start.36
  667.3 7.3 copy-start.37
  667.3 93.3 %copy-start.5 = (f32[256,1024]{1,0:T(8,128)S(1)}, f32[256,1024]{1,0:T(8,128)}, u32[]{:S(2)}) copy-start(f32[256,1024]{1,0:T(8,128)} %copy-done.4) | copy-start | bytes 3145732
  667.3 93.3 %copy-start.34 = (f32[256]{0:T(256)S(1)}, f32[256]{0:T(256)}, u32[]{:S(2)}) copy-start(f32[256]{0:T(256)} %copy-done.33) | copy-start | bytes 3076
  1328.5 6.9 copy-start.17
  1328.5 8.2 slice-start.2
  1328.5 8.7 slice-start.3
  1335.4 6.0 slice-start
  1337.2 5.8 slice-start.1
Sparse Core Ops, SparseCore 0:
  9.6 19.4 all-gather.16
  30.6 21.0 all-gather.26
  55.0 113.8 all-gather.18
  171.6 110.9 all-gather.20
  283.9 8.7 all-gather.22
  294.1 21.0 all-gather.24
  318.5 114.1 all-gather.28
  435.4 115.9 all-gather.30
  553.7 11.5 reduce-scatter.6
  567.5 27.5 reduce-scatter.8
  597.4 27.5 reduce-scatter.10
  632.7 21.7 reduce-scatter.4
  662.0 666.4 all-reduce.13
where the time goes:
time: 1360 us; the launch traced here: 1350 us
  waiting for transfers between devices  829 us (61%)
  matrix products  212 us (16%)
  blocking collectives  187 us (14%)
  local copies, waits for them, and re-layouts  80.3 us (6%)
  other arithmetic  27.8 us (2%)
  between operations  16.2 us (1%)
    psum x1, waiting for transfers between devices, local(): lax.psum((part_gain_one, part_shift_one, part_qkv, part_query, part_value...  567 us
    all_gather x1, waiting for transfers between devices, local(): key_piece = lax.all_gather(keys, 'ctx', axis=1, tiled=True)  107 us
    all_gather x1, waiting for transfers between devices, local(): value_piece = lax.all_gather(values, 'ctx', axis=1, tiled=True)  102 us
    psum x1, blocking collectives, local(): lax.psum((part_gain_one, part_shift_one, part_qkv, part_query, part_value...  81.7 us
    all_gather x1, blocking collectives, local(): lax.all_gather(row_delta.transpose(0, 2, 1), 'ctx', axis=1, tiled=True)  43 us
    all_gather x1, blocking collectives, local(): lax.all_gather(row_lse.transpose(0, 2, 1), 'ctx', axis=1, tiled=True)  42 us
    dot_general x4, matrix products, inner(): lax.dot_general(left, right, (((0,), (0,)), ((), ())), preferred_element_...  30.3 us
    dot_general x1, matrix products, local(): jnp.einsum('sphe,sbhe->shpb', grad_part, value_heads, preferred_element_t...  28.4 us
  transfers between devices with their start and end apart: 13, of which 7 were waited for; matrix products, arithmetic and copies ran while one was open for 22% of the time, Pallas kernels for 0%

commit v1 on v0

v1 whole, which is shorter than its diff:
```python
from functools import partial
import math

import jax
import jax.numpy as jnp
from jax import lax
from jax.experimental import pallas as pl
from jax.experimental.pallas import tpu as pltpu
from jax.sharding import PartitionSpec as P

HEADS = 16


def norm(inputs, gain, shift):
    mean = jnp.mean(inputs, axis=-1, keepdims=True)
    centred = inputs - mean
    spread = jnp.mean(centred * centred, axis=-1, keepdims=True)
    return centred * lax.rsqrt(spread + 1e-05) * gain + shift


def inner(left, right):
    return lax.dot_general(
        left, right, (((0,), (0,)), ((), ())), preferred_element_type=jnp.float32
    )


def times_transposed(left, right):
    return lax.dot_general(
        left, right, (((1,), (1,)), ((), ())), preferred_element_type=jnp.float32
    )


def dot_nt(left, right):
    return lax.dot_general(
        left, right, (((1,), (1,)), ((), ())), preferred_element_type=jnp.float32
    )


def dot_nn(left, right):
    return jnp.dot(left, right, preferred_element_type=jnp.float32)


def causal(scores_t, start):
    rows, size = scores_t.shape
    key = lax.broadcasted_iota(jnp.int32, (size, size), 0)
    pos = lax.broadcasted_iota(jnp.int32, (size, size), 1)
    last = jnp.where(key <= pos, scores_t[start:], -1e30)
    if start == 0:
        return last
    return jnp.concatenate([scores_t[:start], last], axis=0)


def forward_kernel(head_size, size, packed_ref, out_ref, keep_ref, lse_ref):
    chips, _, block, span = packed_ref.shape
    length = chips * block
    query = packed_ref[:, 0].reshape(length, span)
    keys = packed_ref[:, 1].reshape(length, span)
    values = packed_ref[:, 2].reshape(length, span)
    for first in range(0, length, size):
        stop = first + size
        parts = []
        for head in range(span // head_size):
            cols = slice(head * head_size, (head + 1) * head_size)
            scores = causal(dot_nt(keys[:stop, cols], query[first:stop, cols]), first)
            top = jnp.max(scores, axis=0, keepdims=True)
            weights = jnp.exp(scores - top)
            total = jnp.sum(weights, axis=0, keepdims=True)
            summed = lax.dot_general(
                values[:stop, cols],
                weights.astype(jnp.bfloat16),
                (((0,), (0,)), ((), ())),
                preferred_element_type=jnp.float32,
            )
            attended = summed / total
            keep_ref[head, :, first:stop] = attended
            lse_ref[head, :, first:stop] = top + jnp.log(total)
            parts.append(attended)
        joined = parts[0] if len(parts) == 1 else jnp.concatenate(parts, axis=0)
        out_ref[first // block : stop // block] = (
            joined.T.astype(jnp.bfloat16).reshape(size // block, block, span)
        )


def backward_kernel(head_size, size, packed_ref, grad_ref, keep_ref, lse_ref, out_ref, key_acc, value_acc):
    chips, _, block, span = packed_ref.shape
    length = chips * block
    query = packed_ref[:, 0].reshape(length, span)
    keys = packed_ref[:, 1].reshape(length, span)
    values = packed_ref[:, 2].reshape(length, span)
    grads = grad_ref[...].reshape(length, span)
    key_acc[...] = jnp.zeros_like(key_acc)
    value_acc[...] = jnp.zeros_like(value_acc)
    for first in range(0, length, size):
        stop = first + size
        grad_t = grads[first:stop].astype(jnp.float32).T
        parts = []
        for head in range(span // head_size):
            cols = slice(head * head_size, (head + 1) * head_size)
            q, do = query[first:stop, cols], grads[first:stop, cols]
            k, v = keys[:stop, cols], values[:stop, cols]
            delta = jnp.sum(grad_t[cols] * keep_ref[head, :, first:stop], axis=0, keepdims=True)
            scores = causal(dot_nt(k, q), first)
            probs = jnp.exp(scores - lse_ref[head, :, first:stop])
            value_acc[head, :stop] += dot_nn(probs.astype(jnp.bfloat16), do)
            slopes = (probs * (dot_nt(v, do) - delta)).astype(jnp.bfloat16)
            key_acc[head, :stop] += dot_nn(slopes, q)
            parts.append(
                lax.dot_general(
                    k, slopes, (((0,), (0,)), ((), ())), preferred_element_type=jnp.float32
                )
            )
        joined = parts[0] if len(parts) == 1 else jnp.concatenate(parts, axis=0)
        grad_query = (joined * (1.0 / math.sqrt(head_size))).T
        out_ref[first // block : stop // block, 0] = (
            grad_query.astype(jnp.bfloat16).reshape(size // block, block, span)
        )
    for at, acc in ((1, key_acc), (2, value_acc)):
        heads = [acc[head] for head in range(span // head_size)]
        whole = heads[0] if len(heads) == 1 else jnp.concatenate(heads, axis=1)
        out_ref[:, at] = whole.astype(jnp.bfloat16).reshape(chips, block, span)


def attend_forward(packed, head_size):
    chips, _, block, span = packed.shape
    length, heads = chips * block, span // head_size
    pairs = heads * length * length
    return pl.pallas_call(
        partial(forward_kernel, head_size, min(512, length)),
        out_shape=(
            jax.ShapeDtypeStruct((chips, block, span), jnp.bfloat16),
            jax.ShapeDtypeStruct((heads, head_size, length), jnp.float32),
            jax.ShapeDtypeStruct((heads, 1, length), jnp.float32),
        ),
        compiler_params=pltpu.CompilerParams(vmem_limit_bytes=56 * 2**20),
        cost_estimate=pl.CostEstimate(
            flops=3 * pairs * head_size, bytes_accessed=6 * packed.size, transcendentals=pairs
        ),
        name="attend_forward",
    )(packed)


def attend_backward(packed, grads, kept, lse, head_size):
    chips, _, block, span = packed.shape
    length, heads = chips * block, span // head_size
    pairs = heads * length * length
    return pl.pallas_call(
        partial(backward_kernel, head_size, min(512, length)),
        out_shape=jax.ShapeDtypeStruct(packed.shape, jnp.bfloat16),
        scratch_shapes=[
            pltpu.VMEM((heads, length, head_size), jnp.float32),
            pltpu.VMEM((heads, length, head_size), jnp.float32),
        ],
        compiler_params=pltpu.CompilerParams(vmem_limit_bytes=56 * 2**20),
        cost_estimate=pl.CostEstimate(
            flops=8 * pairs * head_size, bytes_accessed=8 * packed.size, transcendentals=pairs
        ),
        name="attend_backward",
    )(packed, grads, kept, lse)


def to_heads(arrays, chips):
    seqs, block, width = arrays[0].shape
    span = seqs * width // chips
    parts = [
        item.reshape(seqs, block, width // span, span)
        .transpose(0, 2, 1, 3)
        .reshape(chips, block, span)
        for item in arrays
    ]
    return lax.all_to_all(jnp.stack(parts, axis=1), "ctx", 0, 0, tiled=True)


def to_tokens(item, seqs, width):
    chips, count, block, span = item.shape
    back = lax.all_to_all(item, "ctx", 0, 0, tiled=True)
    back = back.reshape(seqs, width // span, count, block, span).transpose(2, 0, 3, 1, 4)
    return back.reshape(count, seqs * block, width)


def reduce_rows(grad):
    part = lax.psum_scatter(grad.astype(jnp.bfloat16), "fsdp", scatter_dimension=0, tiled=True)
    part = lax.psum_scatter(part, "ctx", scatter_dimension=0, tiled=True)
    return lax.all_gather(part, "ctx", axis=0, tiled=True)


def local(
    tokens,
    grad_out,
    ln1_gain,
    ln1_bias,
    w_qkv,
    b_query,
    b_value,
    w_out,
    b_out,
    ln2_gain,
    ln2_bias,
    w_fc,
    b_fc,
    w_proj,
    b_proj,
):
    fsdp = lax.axis_size("fsdp")
    chips = lax.axis_size("ctx")
    vectors = (ln1_gain, ln1_bias, b_query, b_value, b_out, ln2_gain, ln2_bias, b_proj, b_fc)
    edges = [0]
    for item in vectors:
        edges.append(edges[-1] + item.shape[0])
    wide_qkv = lax.all_gather(w_qkv, "fsdp", axis=0, tiled=True)
    joined = lax.all_gather(jnp.concatenate(vectors).reshape(-1, 128), "fsdp", axis=0, tiled=True)
    joined = joined.reshape(fsdp, edges[-1])
    (gain_one, shift_one, bias_query, bias_value, bias_out, gain_two, shift_two, bias_proj, bias_fc) = (
        joined[:, at:to].reshape(-1) for at, to in zip(edges[:-1], edges[1:])
    )
    wide_out = lax.all_gather(w_out, "fsdp", axis=0, tiled=True)
    wide_fc = lax.all_gather(w_fc, "fsdp", axis=0, tiled=True)
    wide_proj = lax.all_gather(w_proj, "fsdp", axis=0, tiled=True)
    gain_one = gain_one.astype(jnp.float32)
    shift_one = shift_one.astype(jnp.float32)
    gain_two = gain_two.astype(jnp.float32)
    shift_two = shift_two.astype(jnp.float32)
    seqs, block, width = tokens.shape
    rows = seqs * block
    heads = HEADS
    head_size = width // heads
    scale = 1.0 / math.sqrt(head_size)
    inputs = tokens.astype(jnp.float32).reshape(rows, width)
    low_one = norm(inputs, gain_one, shift_one).astype(jnp.bfloat16)
    packed = jnp.dot(low_one, wide_qkv, preferred_element_type=jnp.float32)
    query = (packed[:, :width] + bias_query.astype(jnp.float32)).astype(jnp.bfloat16)
    keys = packed[:, width : 2 * width].astype(jnp.bfloat16)
    values = (packed[:, 2 * width :] + bias_value.astype(jnp.float32)).astype(jnp.bfloat16)
    query = query * jnp.asarray(scale, jnp.bfloat16)
    shape = (seqs, block, width)
    packed_heads = to_heads(
        (query.reshape(shape), keys.reshape(shape), values.reshape(shape)), chips
    )
    attended, kept, row_lse = attend_forward(packed_heads, head_size)
    low_att = to_tokens(attended[:, None], seqs, width)[0]
    mixed = (
        inputs
        + jnp.dot(low_att, wide_out, preferred_element_type=jnp.float32)
        + bias_out.astype(jnp.float32)
    )
    low_two = norm(mixed, gain_two, shift_two).astype(jnp.bfloat16)
    hidden = jnp.dot(low_two, wide_fc, preferred_element_type=jnp.float32) + bias_fc.astype(
        jnp.float32
    )
    low_act = jax.nn.gelu(hidden, approximate=True).astype(jnp.bfloat16)
    result = (
        mixed
        + jnp.dot(low_act, wide_proj, preferred_element_type=jnp.float32)
        + bias_proj.astype(jnp.float32)
    )
    output = result.astype(jnp.bfloat16).reshape(seqs, block, width)
    grad_rows = grad_out.reshape(rows, width)
    grad_float = grad_rows.astype(jnp.float32)
    grad_b_proj = jnp.sum(grad_float, axis=0)
    grad_w_proj = inner(low_act, grad_rows)
    grad_act = times_transposed(grad_rows, wide_proj)
    _, gelu_back = jax.vjp(partial(jax.nn.gelu, approximate=True), hidden)
    low_hidden = gelu_back(grad_act)[0].astype(jnp.bfloat16)
    grad_b_fc = jnp.sum(low_hidden.astype(jnp.float32), axis=0)
    grad_w_fc = inner(low_two, low_hidden)
    grad_normed_two = times_transposed(low_hidden, wide_fc)
    _, norm_two_back = jax.vjp(norm, mixed, gain_two, shift_two)
    grad_mixed_part, grad_ln2_gain, grad_ln2_bias = norm_two_back(grad_normed_two)
    grad_mixed = grad_float + grad_mixed_part
    low_branch = grad_mixed.astype(jnp.bfloat16)
    grad_b_out = jnp.sum(low_branch.astype(jnp.float32), axis=0)
    grad_w_out = inner(low_att, low_branch)
    low_grad_att = times_transposed(low_branch, wide_out).astype(jnp.bfloat16).reshape(shape)
    grad_heads = to_heads((low_grad_att,), chips)[:, 0]
    grads = attend_backward(packed_heads, grad_heads, kept, row_lse, head_size)
    low_grad_query, low_grad_keys, low_grad_values = to_tokens(grads, seqs, width)
    grad_b_query = jnp.sum(low_grad_query.astype(jnp.float32), axis=0)
    grad_b_value = jnp.sum(low_grad_values.astype(jnp.float32), axis=0)
    grad_packed = jnp.concatenate([low_grad_query, low_grad_keys, low_grad_values], axis=1)
    grad_w_qkv = inner(low_one, grad_packed)
    grad_normed_one = times_transposed(grad_packed, wide_qkv)
    _, norm_one_back = jax.vjp(norm, inputs, gain_one, shift_one)
    grad_input_part, grad_ln1_gain, grad_ln1_bias = norm_one_back(grad_normed_one)
    grad_tokens = (grad_mixed + grad_input_part).astype(jnp.bfloat16).reshape(seqs, block, width)
    small = (
        grad_ln1_gain,
        grad_ln1_bias,
        grad_b_query,
        grad_b_value,
        grad_b_out,
        grad_ln2_gain,
        grad_ln2_bias,
        grad_b_proj,
        grad_b_fc,
    )
    small = jnp.concatenate([item.reshape(fsdp, -1) for item in small], axis=1)
    small = small.reshape(fsdp, -1, 128)
    spare = -small.shape[1] % (16 * chips)
    small = jnp.pad(small, ((0, 0), (0, spare), (0, 0)))
    out_rows = w_out.size // 128
    tail = jnp.concatenate([grad_w_out.reshape(fsdp, out_rows, 128), small], axis=1)
    tail = reduce_rows(tail.reshape(-1, 128)).astype(jnp.float32)
    total_out = tail[:out_rows].reshape(w_out.shape)
    rest = tail[out_rows:].reshape(-1)
    part = [rest[at:to] for at, to in zip(edges[:-1], edges[1:])]
    total_qkv = reduce_rows(grad_w_qkv).astype(jnp.float32)
    total_fc = reduce_rows(grad_w_fc).astype(jnp.float32)
    total_proj = reduce_rows(grad_w_proj).astype(jnp.float32)
    return (
        output,
        grad_tokens,
        part[0],
        part[1],
        total_qkv,
        part[2],
        part[3],
        total_out,
        part[4],
        part[5],
        part[6],
        total_fc,
        part[8],
        total_proj,
        part[7],
    )


def solution(mesh):
    in_specs = (
        P("fsdp", "ctx", None),
        P("fsdp", "ctx", None),
        P("fsdp"),
        P("fsdp"),
        P("fsdp", None),
        P("fsdp"),
        P("fsdp"),
        P("fsdp", None),
        P("fsdp"),
        P("fsdp"),
        P("fsdp"),
        P("fsdp", None),
        P("fsdp"),
        P("fsdp", None),
        P("fsdp"),
    )
    out_specs = (
        P("fsdp", "ctx", None),
        P("fsdp", "ctx", None),
        P("fsdp"),
        P("fsdp"),
        P("fsdp", None),
        P("fsdp"),
        P("fsdp"),
        P("fsdp", None),
        P("fsdp"),
        P("fsdp"),
        P("fsdp"),
        P("fsdp", None),
        P("fsdp"),
        P("fsdp", None),
        P("fsdp"),
    )
    return jax.shard_map(local, mesh=mesh, in_specs=in_specs, out_specs=out_specs, check_vma=False)
```

time: 1360 us -> 996 us (0.73)
  matrix products: 212 us -> 69.4 us
  blocking collectives: 187 us -> 65 us
  waiting for transfers between devices: 829 us -> 758 us
  local copies, waits for them, and re-layouts: 80.3 us -> 18.6 us
  Pallas kernels: 0 us -> 27.4 us
    psum x1 -> x0, waiting for transfers between devices: 567 us -> none  [local(): lax.psum((part_gain_one, part_shift_one, part_qkv, part_query, part_value...]
    reduce_scatter x4 -> x8, waiting for transfers between devices: 21.6 us -> 455 us  [the longest x4 407 us: reduce_rows(): part = lax.psum_scatter(part, 'ctx', scatter_dimension=0, tiled=True)]
    dot_general x7 -> x0, matrix products: 135 us -> none  [the longest x1 28.4 us: local(): jnp.einsum('sphe,sbhe->shpb', grad_part, value_heads, preferred_element_t...]
    all_gather x11 -> x1, blocking collectives: 101 us -> 1.93 us  [local(): lax.all_gather(jnp.concatenate(vectors).reshape(-1, 128), 'fsdp', axis=0,...]
    psum x1 -> x0, blocking collectives: 81.7 us -> none  [local(): lax.psum((part_gain_one, part_shift_one, part_qkv, part_query, part_value...]
    all_to_all x0 -> x2, blocking collectives: none -> 63 us  [to_heads(): return lax.all_to_all(jnp.stack(parts, axis=1), 'ctx', 0, 0, tiled=True)]
    all_gather x4 -> x0, local copies, waits for them, and re-layouts: 47.4 us -> none  [the longest x1 12.1 us: local(): grad_piece = lax.all_gather(low_grad_att, 'ctx', axis=1, tiled=True)]
    all_to_all x0 -> x2, waiting for transfers between devices: none -> 32 us  [to_tokens(): back = lax.all_to_all(item, 'ctx', 0, 0, tiled=True)]
  transfers between devices with their start and end apart: 13 -> 18, of which waited for: 7 -> 14; matrix products, arithmetic and copies ran while one was open for 22% -> 8% of each run, Pallas kernels for 0% -> 1%
where the time goes in v1:
time: 996 us; the launch traced here: 990 us
  waiting for transfers between devices  758 us (76%)
  matrix products  69.4 us (7%)
  blocking collectives  65 us (7%)
  Pallas kernels  27.4 us (3%)
  other arithmetic  26.6 us (3%)
  local copies, waits for them, and re-layouts  18.6 us (2%)
  between operations  15 us (2%)
    reduce_scatter x4, waiting for transfers between devices, reduce_rows(): part = lax.psum_scatter(part, 'ctx', scatter_dimension=0, tiled=True)  407 us
    all_gather x4, waiting for transfers between devices, reduce_rows(): return lax.all_gather(part, 'ctx', axis=0, tiled=True)  254 us
    all_to_all x2, blocking collectives, to_heads(): return lax.all_to_all(jnp.stack(parts, axis=1), 'ctx', 0, 0, tiled=True)  63 us
    reduce_scatter x4, waiting for transfers between devices, reduce_rows(): lax.psum_scatter(grad.astype(jnp.bfloat16), 'fsdp', scatter_dimension=0,...  47.9 us
    all_to_all x2, waiting for transfers between devices, to_tokens(): back = lax.all_to_all(item, 'ctx', 0, 0, tiled=True)  32 us
    dot_general x4, matrix products, inner(): lax.dot_general(left, right, (((0,), (0,)), ((), ())), preferred_element_...  26 us
  transfers between devices with their start and end apart: 18, of which 14 were waited for; matrix products, arithmetic and copies ran while one was open for 8% of the time, Pallas kernels for 1%

profile of v1, /device:TPU:0, one launch (start us, length us, event | category | flops | bytes accessed | tf_op | source)
XLA Modules:
  0.0 990.2 jit_solution(10728637029392249504)
XLA Ops:
  7.2 0.7 all-gather.9.cloned.1.call-update
  8.1 0.7 all-gather.15.cloned.1.call-update
  8.8 0.7 all-gather.11.cloned.1.call-update
  9.5 0.5 all-gather.13.cloned.1.call-update
  10.1 0.3 dynamic-update-slice.12
  10.4 0.2 dynamic-update-slice.13
  11.5 0.2 dynamic-update-slice.18
  11.9 1.9 all_gather.27
  14.1 0.3 multiply_reduce_fusion.5
  14.4 0.3 add_convert_fusion.2
  14.7 14.4 %all-gather.9.cloned.1.call-done = bf16[1024,3072]{1,0:T(8,128)(2,1)} async-done(((bf16[512,3072]{1,0:T(8,128)(2,1)}), bf16[1024,3072]{1,0:T(8,128)(2,1)}) %all-gather.9.cloned.1.call-update) | async-done | bytes 6291472 | tf_op jit(solution)/shard_map/all_gather | solution.py:209
  29.1 4.6 fusion.34
  34.1 0.3 fusion.17
  34.9 44.9 %all_to_all.20.packed_ref = bf16[16,3,128,128]{3,2,1,0:T(8,128)(2,1)} all-to-all(bf16[16,3,128,128]{3,2,1,0:T(8,128)(2,1)S(1)} %pad_maximum_fusion), channel_id=1, replica_groups=mesh['ctx'=16,'fsdp'=2] {'ctx'}, dimensions={0} | all-to-all | bytes 3145728 | tf_op jit(solution)/shard_map/all_to_all | solution.py:170
  79.8 10.1 %attend_forward.1 = (bf16[16,128,128]{2,1,0:T(8,128)(2,1)}, f32[2,64,2048]{2,1,0:T(8,128)}, f32[2,1,2048]{2,1,0:T(1,128)}) custom-call(bf16[16,3,128,128]{3,2,1,0:T(8,128)(2,1)} %all_to_all.20.packed_ref), custom_call_target="tpu_custom_call" | custom-call | flops 1610612736 | bytes 4718592 | tf_op jit(solution)/shard_map/attend_forward/pallas_call | solution.py:127
  90.0 4.7 all-to-all-start.1
  94.7 7.8 fusion.35
  102.5 6.6 all-to-all-done.1
  109.1 0.3 copy.44
  109.4 2.6 fusion.33
  112.0 0.3 multiply_reduce_fusion.4
  112.3 11.4 %fusion.28 = (bf16[4096]{0:T(1024)(128)(2,1)S(1)}, bf16[256,4096]{1,0:T(8,128)(2,1)S(1)}, f32[256,4096]{1,0:T(8,128)}) fusion(f32[256,4096]{1,0:T(8,128)} %fusion.35, f32[4096]{0:T(1024)S(1)} %bitcast.197, bf16[1024,4096]{1,0:T(8,128)(2,1)} %all-gather.13.cloned.1.call-done, f32[256,1024]{1,0:T(8,128)S(1)} %get-tuple-element.60, f32[1024]{0:T(1024)S(1)} %bitcast.186, ...), kind=kOutput, calls=%fused_computation.104 | convolution fusion | flops 2171858944 | bytes 19957760 | tf_op jit(solution)/shard_map/dot_general | solution.py:246
  123.8 2.7 multiply_reduce_fusion
  126.5 0.4 fusion.32
  126.9 0.2 fusion.30
  127.1 0.8 copy-done.8
  128.0 0.7 fusion.12
  129.0 18.1 %all_to_all.21 = bf16[16,1,128,128]{3,2,1,0:T(8,128)(2,1)} all-to-all(bf16[16,1,128,128]{3,2,1,0:T(8,128)(2,1)S(1)} %bitcast.170), channel_id=1, replica_groups=mesh['ctx'=16,'fsdp'=2] {'ctx'}, dimensions={0} | all-to-all | bytes 1048576 | tf_op jit(solution)/shard_map/all_to_all | solution.py:170
  147.1 17.3 %attend_backward.1 = bf16[16,3,128,128]{3,2,1,0:T(8,128)(2,1)} custom-call(bf16[16,3,128,128]{3,2,1,0:T(8,128)(2,1)} %all_to_all.20.packed_ref, bf16[16,128,128]{2,1,0:T(8,128)(2,1)} %bitcast.180, f32[2,64,2048]{2,1,0:T(8,128)} %get-tuple-element.19.keep_ref, f32[2,1,2048]{2,1,0:T(1,128)} %get-tuple-element.20.lse_ref), custom_call_target="tpu_custom_call" | custom-call | flops 4294967296 | bytes 6291456 | tf_op jit(solution)/shard_map/attend_backward/pallas_call | solution.py:146
  164.4 4.4 all-to-all-start.3
  169.1 3.3 convolution_convert_fusion.3
  172.3 4.2 reshape.287
  176.5 25.4 %all-to-all-done.3 = bf16[16,3,128,128]{3,2,1,0:T(8,128)(2,1)} async-done(((bf16[16,3,128,128]{3,2,1,0:T(8,128)(2,1)}), bf16[16,3,128,128]{3,2,1,0:T(8,128)(2,1)}, u32[]{:S(2)}, u32[]{:S(2)}) %all-to-all-start.3) | async-done | bytes 1572896 | tf_op jit(solution)/shard_map/all_to_all | solution.py:175
  201.9 2.4 copy.80
  204.3 0.4 slice_reduce_fusion
  204.9 5.3 fusion.27
  210.3 1.0 copy-done.3
  211.3 0.6 multiply_reduce_fusion.1
  212.0 3.1 fusion.8
  215.2 6.1 convolution_convert_fusion.2
  221.4 7.6 convolution_convert_fusion.1
  229.0 0.3 reduce-scatter.21.cloned.1.call-start
  229.3 9.0 convolution_convert_fusion
  238.5 0.7 reduce-scatter.11.cloned.1.call-update
  239.2 6.1 reduce-scatter.13.cloned.1.call-done
  245.4 20.8 %reduce-scatter.17.cloned.1.call-done = bf16[512,4096]{1,0:T(8,128)(2,1)} async-done(((bf16[1024,4096]{1,0:T(8,128)(2,1)}), bf16[512,4096]{1,0:T(8,128)(2,1)}) %reduce-scatter.17.cloned.1.call-update) | async-done | bytes 4194320 | tf_op jit(solution)/shard_map/reduce_scatter | solution.py:181
  266.3 21.0 %reduce-scatter.21.cloned.1.call-done = bf16[2048,1024]{1,0:T(8,128)(2,1)} async-done(((bf16[4096,1024]{1,0:T(8,128)(2,1)}), bf16[2048,1024]{1,0:T(8,128)(2,1)}) %reduce-scatter.21.cloned.1.call-update) | async-done | bytes 4194320 | tf_op jit(solution)/shard_map/reduce_scatter | solution.py:181
  287.3 81.6 %reduce-scatter.11.cloned.1.call-done = bf16[272,128]{1,0:T(8,128)(2,1)} async-done(((bf16[4352,128]{1,0:T(8,128)(2,1)}), bf16[272,128]{1,0:T(8,128)(2,1)}) %reduce-scatter.11.cloned.1.call-update) | async-done | bytes 69648 | tf_op jit(solution)/shard_map/reduce_scatter | solution.py:182
  368.9 131.7 %reduce-scatter.15.cloned.1.call-done = bf16[32,3072]{1,0:T(8,128)(2,1)} async-done(((bf16[512,3072]{1,0:T(8,128)(2,1)}), bf16[32,3072]{1,0:T(8,128)(2,1)}) %reduce-scatter.15.cloned.1.call-update) | async-done | bytes 196624 | tf_op jit(solution)/shard_map/reduce_scatter | solution.py:182
  500.7 96.6 %reduce-scatter.19.cloned.1.call-done = bf16[32,4096]{1,0:T(8,128)(2,1)} async-done(((bf16[512,4096]{1,0:T(8,128)(2,1)}), bf16[32,4096]{1,0:T(8,128)(2,1)}) %reduce-scatter.19.cloned.1.call-update) | async-done | bytes 262160 | tf_op jit(solution)/shard_map/reduce_scatter | solution.py:182
  597.4 96.8 %reduce-scatter.23.cloned.1.call-done = bf16[128,1024]{1,0:T(8,128)(2,1)} async-done(((bf16[2048,1024]{1,0:T(8,128)(2,1)}), bf16[128,1024]{1,0:T(8,128)(2,1)}) %reduce-scatter.23.cloned.1.call-update) | async-done | bytes 262160 | tf_op jit(solution)/shard_map/reduce_scatter | solution.py:182
  694.3 8.3 fusion.11
  702.5 1.3 add_convert_fusion
  703.8 48.6 %all-gather.17.cloned.1.call-done = bf16[4352,128]{1,0:T(8,128)(2,1)} async-done(((bf16[272,128]{1,0:T(8,128)(2,1)}), bf16[4352,128]{1,0:T(8,128)(2,1)}) %all-gather.17.cloned.1.call-update) | async-done | bytes 1114128 | tf_op jit(solution)/shard_map/all_gather | solution.py:183
  752.4 2.8 slice.154
  755.2 2.7 reshape.298
  758.0 0.6 slice_bitcast_fusion
  758.7 0.6 slice_bitcast_fusion.1
  759.3 62.8 %all-gather.19.cloned.1.call-done = bf16[512,3072]{1,0:T(8,128)(2,1)} async-done(((bf16[32,3072]{1,0:T(8,128)(2,1)}), bf16[512,3072]{1,0:T(8,128)(2,1)}) %all-gather.19.cloned.1.call-update) | async-done | bytes 3145744 | tf_op jit(solution)/shard_map/all_gather | solution.py:183
  822.1 5.4 convert_element_type.209
  827.5 71.8 %all-gather.21.cloned.1.call-done = bf16[512,4096]{1,0:T(8,128)(2,1)} async-done(((bf16[32,4096]{1,0:T(8,128)(2,1)}), bf16[512,4096]{1,0:T(8,128)(2,1)}) %all-gather.21.cloned.1.call-update) | async-done | bytes 4194320 | tf_op jit(solution)/shard_map/all_gather | solution.py:183
  899.3 6.7 convert_element_type.211
  906.0 70.7 %all-gather.23.cloned.1.call-done = bf16[2048,1024]{1,0:T(8,128)(2,1)} async-done(((bf16[128,1024]{1,0:T(8,128)(2,1)}), bf16[2048,1024]{1,0:T(8,128)(2,1)}) %all-gather.23.cloned.1.call-update) | async-done | bytes 4194320 | tf_op jit(solution)/shard_map/all_gather | solution.py:183
  976.6 6.6 convert_element_type.213
  (133 shorter events, 4.2 us)
Async XLA Ops:
  7.2 21.9 %all-gather.9.cloned.1.call-start = ((), (), s32[]{:S(2)}) async-start(), calls=%async_computation.12 | async-start | bytes 9437184 | tf_op jit(solution)/shard_map/all_gather | solution.py:209
  7.9 2.2 copy-start.11
  7.9 2.4 copy-start.12
  7.9 2.6 copy-start.13
  7.9 2.8 copy-start.14
  8.0 3.1 copy-start.15
  8.0 3.3 copy-start.16
  8.0 3.5 copy-start.17
  8.0 3.7 copy-start.18
  8.0 3.9 copy-start.10
  8.0 5.9 copy-start
  8.0 86.7 %all-gather.15.cloned.1.call-start = ((), (), s32[]{:S(2)}) async-start(), calls=%async_computation.15 | async-start | bytes 12582912 | tf_op jit(solution)/shard_map/all_gather | solution.py:217
  8.8 100.7 %all-gather.11.cloned.1.call-start = ((), (), s32[]{:S(2)}) async-start(), calls=%async_computation.13 | async-start | bytes 3145728 | tf_op jit(solution)/shard_map/all_gather | solution.py:215
  9.5 102.8 %all-gather.13.cloned.1.call-start = ((), (), s32[]{:S(2)}) async-start(), calls=%async_computation.14 | async-start | bytes 12582912 | tf_op jit(solution)/shard_map/all_gather | solution.py:216
  14.7 19.0 %copy-start.6 = (bf16[256,1024]{1,0:T(8,128)(2,1)}, bf16[256,1024]{1,0:T(8,128)(2,1)S(1)}, u32[]{:S(2)}) copy-start(bf16[256,1024]{1,0:T(8,128)(2,1)S(1)} %add_convert_fusion.2) | copy-start | bytes 1572868
  79.8 14.9 %copy-start.2 = (bf16[2,128,1024]{2,1,0:T(8,128)(2,1)S(1)}, bf16[2,128,1024]{2,1,0:T(8,128)(2,1)}, u32[]{:S(2)}) copy-start(bf16[2,128,1024]{2,1,0:T(8,128)(2,1)} %param.16) | copy-start | bytes 1572868
  90.0 19.1 %all-to-all-start.1 = ((bf16[16,1,128,128]{3,2,1,0:T(8,128)(2,1)}), bf16[16,1,128,128]{3,2,1,0:T(8,128)(2,1)S(1)}, u32[]{:S(2)}, u32[]{:S(2)}) async-start(bf16[16,1,128,128]{3,2,1,0:T(8,128)(2,1)} %bitcast.179), calls=%async_computation.1 | async-start | bytes 1048576 | tf_op jit(solution)/shard_map/all_to_all | solution.py:175
  109.4 14.4 %copy-start.9 = (bf16[2,8,1,128,128]{4,1,3,0,2:T(8,128)(2,1)}, bf16[2,8,1,128,128]{4,1,3,0,2:T(8,128)(2,1)S(1)}, u32[]{:S(2)}) copy-start(bf16[2,8,1,128,128]{4,1,3,0,2:T(8,128)(2,1)S(1)} %copy.44) | copy-start | bytes 1572868
  112.3 11.5 %copy-start.19 = (bf16[1024,4096]{1,0:T(8,128)(2,1)S(1)}, bf16[1024,4096]{1,0:T(8,128)(2,1)}, u32[]{:S(2)}) copy-start(bf16[1024,4096]{1,0:T(8,128)(2,1)} %all-gather.13.cloned.1.call-done) | copy-start | bytes 25165828
  123.8 2.7 copy-start.7
  126.5 1.6 copy-start.20
  127.1 0.8 copy-start.8
  164.4 37.5 %all-to-all-start.3 = ((bf16[16,3,128,128]{3,2,1,0:T(8,128)(2,1)}), bf16[16,3,128,128]{3,2,1,0:T(8,128)(2,1)}, u32[]{:S(2)}, u32[]{:S(2)}) async-start(bf16[16,3,128,128]{3,2,1,0:T(8,128)(2,1)} %attend_backward.1), calls=%async_computation.3 | async-start | bytes 3145728 | tf_op jit(solution)/shard_map/all_to_all | solution.py:175
  168.8 69.6 %reduce-scatter.9.cloned.1.call-start = ((), (), s32[]{:S(2)}) async-start(), calls=%async_computation.16 | async-start | bytes 3342336 | tf_op jit(solution)/shard_map/reduce_scatter | solution.py:181
  204.9 5.3 copy-start.5
  210.3 1.0 copy-start.3
  215.2 30.1 %reduce-scatter.13.cloned.1.call-start = ((), (), s32[]{:S(2)}) async-start(), calls=%async_computation.19 | async-start | bytes 9437184 | tf_op jit(solution)/shard_map/reduce_scatter | solution.py:181
  221.4 44.8 %reduce-scatter.17.cloned.1.call-start = ((), (), s32[]{:S(2)}) async-start(), calls=%async_computation.22 | async-start | bytes 12582912 | tf_op jit(solution)/shard_map/reduce_scatter | solution.py:181
  229.0 58.2 %reduce-scatter.21.cloned.1.call-start = ((), (), s32[]{:S(2)}) async-start(), calls=%async_computation.25 | async-start | bytes 12582912 | tf_op jit(solution)/shard_map/reduce_scatter | solution.py:181
  238.4 130.5 %reduce-scatter.11.cloned.1.call-start = ((), (), s32[]{:S(2)}) async-start(), calls=%async_computation.17 | async-start | bytes 1183744 | tf_op jit(solution)/shard_map/reduce_scatter | solution.py:182
  239.2 261.5 %reduce-scatter.15.cloned.1.call-start = ((), (), s32[]{:S(2)}) async-start(), calls=%async_computation.20 | async-start | bytes 3342336 | tf_op jit(solution)/shard_map/reduce_scatter | solution.py:182
  245.3 352.0 %reduce-scatter.19.cloned.1.call-start = ((), (), s32[]{:S(2)}) async-start(), calls=%async_computation.23 | async-start | bytes 4456448 | tf_op jit(solution)/shard_map/reduce_scatter | solution.py:182
  266.2 428.0 %reduce-scatter.23.cloned.1.call-start = ((), (), s32[]{:S(2)}) async-start(), calls=%async_computation.26 | async-start | bytes 4456448 | tf_op jit(solution)/shard_map/reduce_scatter | solution.py:182
  287.3 465.1 %all-gather.17.cloned.1.call-start = ((), (), s32[]{:S(2)}) async-start(), calls=%async_computation.18 | async-start | bytes 1183744 | tf_op jit(solution)/shard_map/all_gather | solution.py:183
  368.9 453.2 %all-gather.19.cloned.1.call-start = ((), (), s32[]{:S(2)}) async-start(), calls=%async_computation.21 | async-start | bytes 3342336 | tf_op jit(solution)/shard_map/all_gather | solution.py:183
  500.7 398.6 %all-gather.21.cloned.1.call-start = ((), (), s32[]{:S(2)}) async-start(), calls=%async_computation.24 | async-start | bytes 4456448 | tf_op jit(solution)/shard_map/all_gather | solution.py:183
  597.4 379.3 %all-gather.23.cloned.1.call-start = ((), (), s32[]{:S(2)}) async-start(), calls=%async_computation.27 | async-start | bytes 4456448 | tf_op jit(solution)/shard_map/all_gather | solution.py:183
  694.3 8.3 copy-start.4
  752.4 5.5 copy-start.1
Sparse Core Ops, SparseCore 0:
  9.6 19.5 all-gather.8
  30.7 21.0 all-gather.14
  53.3 11.7 all-gather.10
  66.4 21.0 all-gather.12
  215.3 11.4 reduce-scatter.8
  229.6 15.6 reduce-scatter.12
  248.2 17.9 reduce-scatter.16
  269.2 18.0 reduce-scatter.20
  289.5 79.2 reduce-scatter.10
  373.7 126.9 reduce-scatter.14
  503.0 94.3 reduce-scatter.18
  599.5 94.6 reduce-scatter.22
  697.0 55.3 all-gather.16
  755.1 66.9 all-gather.18
  824.7 74.5 all-gather.20
  901.9 74.6 all-gather.22

commit v2 on v1

--- a/solution.py
+++ b/solution.py
@@ -181,6 +181,209 @@
     part = lax.psum_scatter(grad.astype(jnp.bfloat16), "fsdp", scatter_dimension=0, tiled=True)
     part = lax.psum_scatter(part, "ctx", scatter_dimension=0, tiled=True)
     return lax.all_gather(part, "ctx", axis=0, tiled=True)
+
+
+def ring_place(at):
+    z, y, x = at // 4, (at // 2) % 2, at % 2
+    column = y * (3 - x) + (1 - y) * x
+    return column, z
+
+
+def ring_kernel(
+    chips, big, tiny, sum_big, sum_tiny, own, own_tiny, met, met_tiny, hop, hop_tiny,
+    own_sem, met_send, met_recv, hop_send, hop_recv, all_send, all_recv,
+):
+    depth = chips // 4
+    core = lax.axis_index("fsdp")
+    column, z = ring_place(lax.axis_index("ctx"))
+    odd = column % 2
+    place = column * depth + (1 - odd) * z + odd * (depth - 1 - z)
+
+    def device(spot):
+        column, z = spot // depth, spot % depth
+        odd = column % 2
+        z = (1 - odd) * z + odd * (depth - 1 - z)
+        return {"ctx": z * 4 + (column // 2) * 2 + ((column + 1) // 2) % 2}
+
+    after, before = device((place + 1) % chips), device((place + chips - 1) % chips)
+    other = {"fsdp": 1 - core}
+    barrier = pltpu.get_barrier_semaphore()
+    for peer in (after, before, other):
+        pl.semaphore_signal(barrier, inc=1, device_id=peer, device_id_type=pl.DeviceIdType.MESH)
+    pl.semaphore_wait(barrier, 3)
+
+    lanes = big.shape[1]
+    views = []
+    for lane in range(lanes):
+        views.append(
+            (
+                1 - 2 * (lane % 2),
+                lambda half, at, lane=lane: big.at[half, lane, at],
+                own.at[lane],
+                met.at[lane],
+                hop.at[lane],
+                sum_big.at[lane],
+            )
+        )
+    views.append(
+        (1, lambda half, at: tiny.at[half, at], own_tiny, met_tiny, hop_tiny, sum_tiny)
+    )
+
+    def chunk(turn, step):
+        return (place + turn * step + 2 * chips) % chips
+
+    def remote(source, target, send, recv, peer):
+        return pltpu.make_async_remote_copy(
+            src_ref=source,
+            dst_ref=target,
+            send_sem=send,
+            recv_sem=recv,
+            device_id=peer,
+            device_id_type=pl.DeviceIdType.MESH,
+        )
+
+    def fetch(lane, step):
+        turn, source, mine, theirs, _, _ = views[lane]
+        at = chunk(-turn, step)
+        return (
+            pltpu.make_async_copy(source(core, at), mine.at[at], own_sem.at[lane, step]),
+            remote(
+                source(1 - core, at),
+                theirs.at[at],
+                met_send.at[lane, step],
+                met_recv.at[lane, step],
+                other,
+            ),
+        )
+
+    def pass_on(lane, step, source):
+        turn, slots = views[lane][0], views[lane][4]
+        return remote(
+            source,
+            slots.at[step],
+            hop_send.at[lane, step],
+            hop_recv.at[lane, step],
+            after if turn == 1 else before,
+        )
+
+    def share(lane, step):
+        turn, total = views[lane][0], views[lane][5]
+        at = chunk(-turn, step - 1)
+        return remote(
+            total.at[at],
+            total.at[at],
+            all_send.at[lane, step],
+            all_recv.at[lane, step],
+            after if turn == 1 else before,
+        )
+
+    def add(lane, at, target, extra):
+        mine, theirs = views[lane][2].at[at], views[lane][3].at[at]
+
+        def rows(index, carry):
+            span = pl.ds(pl.multiple_of(index * 16, 16), 16)
+            value = mine[span].astype(jnp.float32) + theirs[span].astype(jnp.float32)
+            if extra is not None:
+                value = value + extra[span].astype(jnp.float32)
+            target[span] = value.astype(jnp.bfloat16)
+            return carry
+
+        lax.fori_loop(0, mine.shape[0] // 16, rows, 0)
+
+    every = range(len(views))
+
+    def start(step, carry):
+        for lane in every:
+            for copy in fetch(lane, step):
+                copy.start()
+        return carry
+
+    lax.fori_loop(0, chips, start, 0)
+
+    def ready(lane, step):
+        local_copy, from_other = fetch(lane, step)
+        local_copy.wait()
+        from_other.wait_recv()
+
+    for lane in every:
+        ready(lane, 0)
+        mine = views[lane][2].at[place]
+        add(lane, place, mine, None)
+        pass_on(lane, 0, mine).start()
+
+    def hops(step, carry):
+        for lane in every:
+            slots = views[lane][4]
+            ready(lane, step)
+            pass_on(lane, step - 1, slots.at[step - 1]).wait_recv()
+            add(lane, chunk(-views[lane][0], step), slots.at[step - 1], slots.at[step - 1])
+            pass_on(lane, step, slots.at[step - 1]).start()
+        return carry
+
+    lax.fori_loop(1, chips - 1, hops, 0)
+    for lane in every:
+        slots = views[lane][4]
+        ready(lane, chips - 1)
+        pass_on(lane, chips - 2, slots.at[chips - 2]).wait_recv()
+        at = chunk(-views[lane][0], chips - 1)
+        add(lane, at, views[lane][5].at[at], slots.at[chips - 2])
+        share(lane, 0).start()
+
+    def shares(step, carry):
+        for lane in every:
+            share(lane, step - 1).wait_recv()
+            share(lane, step).start()
+        return carry
+
+    lax.fori_loop(1, chips - 1, shares, 0)
+    for lane in every:
+        share(lane, chips - 2).wait_recv()
+
+    def sent(step, carry):
+        for lane in every:
+            pass_on(lane, step, views[lane][4].at[step]).wait_send()
+            share(lane, step).wait_send()
+            fetch(lane, step)[1].wait_send()
+        return carry
+
+    lax.fori_loop(0, chips - 1, sent, 0)
+    for lane in every:
+        fetch(lane, chips - 1)[1].wait_send()
+
+
+def ring_sum(big, tiny):
+    _, lanes, chips, rows, width = big.shape
+    _, _, low_rows, low_width = tiny.shape
+    whole, low_whole = (lanes, chips, rows, width), (chips, low_rows, low_width)
+    sems = pltpu.SemaphoreType.DMA((lanes + 1, chips))
+    return pl.pallas_call(
+        partial(ring_kernel, chips),
+        out_shape=(
+            jax.ShapeDtypeStruct(whole, jnp.bfloat16),
+            jax.ShapeDtypeStruct(low_whole, jnp.bfloat16),
+        ),
+        in_specs=[pl.BlockSpec(memory_space=pl.ANY)] * 2,
+        out_specs=[pl.BlockSpec(memory_space=pltpu.VMEM)] * 2,
+        scratch_shapes=[
+            pltpu.VMEM(whole, jnp.bfloat16),
+            pltpu.VMEM(low_whole, jnp.bfloat16),
+            pltpu.VMEM(whole, jnp.bfloat16),
+            pltpu.VMEM(low_whole, jnp.bfloat16),
+            pltpu.VMEM((lanes, chips - 1, rows, width), jnp.bfloat16),
+            pltpu.VMEM((chips - 1, low_rows, low_width), jnp.bfloat16),
+        ]
+        + [sems] * 7,
+        compiler_params=pltpu.CompilerParams(
+            collective_id=0, has_side_effects=True, vmem_limit_bytes=58 * 2**20
+        ),
+        name="ring_sum",
+    )(big, tiny)
+
+
+def by_width(grad, fsdp, width):
+    rows, columns = grad.shape
+    cut = grad.astype(jnp.bfloat16).reshape(fsdp, rows // fsdp, columns // width, width)
+    return cut.transpose(0, 2, 1, 3).reshape(fsdp, -1, width)
 
 
 def local(
@@ -294,17 +497,28 @@
     )
     small = jnp.concatenate([item.reshape(fsdp, -1) for item in small], axis=1)
     small = small.reshape(fsdp, -1, 128)
-    spare = -small.shape[1] % (16 * chips)
-    small = jnp.pad(small, ((0, 0), (0, spare), (0, 0)))
-    out_rows = w_out.size // 128
-    tail = jnp.concatenate([grad_w_out.reshape(fsdp, out_rows, 128), small], axis=1)
-    tail = reduce_rows(tail.reshape(-1, 128)).astype(jnp.float32)
-    total_out = tail[:out_rows].reshape(w_out.shape)
-    rest = tail[out_rows:].reshape(-1)
+    grads = (grad_w_fc, grad_w_proj, grad_w_qkv, grad_w_out)
+    shards = (w_fc, w_proj, w_qkv, w_out)
+    if fsdp == 2 and chips % 4 == 0 and w_out.size % (4 * chips * 16) == 0 and chips <= 16:
+        small = small.astype(jnp.bfloat16)
+        spare = -small.shape[1] % (16 * chips)
+        small = jnp.pad(small, ((0, 0), (0, spare), (0, 0))).reshape(fsdp, chips, -1, 128)
+        big = jnp.concatenate([by_width(item, fsdp, width) for item in grads], axis=1)
+        big, rest = ring_sum(big.reshape(fsdp, 4, chips, -1, width), small)
+        big, totals, at = big.reshape(-1, width), [], 0
+        for shard in shards:
+            count = shard.size // width
+            item = big[at : at + count].reshape(-1, shard.shape[0], width).transpose(1, 0, 2)
+            totals.append(item.reshape(shard.shape).astype(jnp.float32))
+            at += count
+        rest = rest.reshape(-1).astype(jnp.float32)
+    else:
+        spare = -small.shape[1] % (16 * chips)
+        small = jnp.pad(small, ((0, 0), (0, spare), (0, 0)))
+        rest = reduce_rows(small.reshape(-1, 128)).reshape(-1).astype(jnp.float32)
+        totals = [reduce_rows(item).astype(jnp.float32) for item in grads]
+    total_fc, total_proj, total_qkv, total_out = totals
     part = [rest[at:to] for at, to in zip(edges[:-1], edges[1:])]
-    total_qkv = reduce_rows(grad_w_qkv).astype(jnp.float32)
-    total_fc = reduce_rows(grad_w_fc).astype(jnp.float32)
-    total_proj = reduce_rows(grad_w_proj).astype(jnp.float32)
     return (
         output,
         grad_tokens,

time: 996 us -> 605 us (0.61)
  waiting for transfers between devices: 758 us -> 23.6 us
  Pallas kernels: 27.4 us -> 299 us
  local copies, waits for them, and re-layouts: 18.6 us -> 88.2 us
  other arithmetic: 26.6 us -> 39.8 us
    reduce_scatter x8 -> x0, waiting for transfers between devices: 455 us -> none  [the longest x4 407 us: reduce_rows(): part = lax.psum_scatter(part, 'ctx', scatter_dimension=0, tiled=True)]
    pallas_call x0 -> x1, Pallas kernels: none -> 271 us  [ring_sum(): pl.pallas_call(partial(ring_kernel, chips), out_shape=(jax.ShapeDtypeStru...]
    all_gather x4 -> x0, waiting for transfers between devices: 254 us -> none  [reduce_rows(): return lax.all_gather(part, 'ctx', axis=0, tiled=True)]
    transpose x0 -> x2, local copies, waits for them, and re-layouts: none -> 25.6 us  [by_width(): return cut.transpose(0, 2, 1, 3).reshape(fsdp, -1, width)]
    all_to_all x2, waiting for transfers between devices: 32 us -> 6.56 us  [to_tokens(): back = lax.all_to_all(item, 'ctx', 0, 0, tiled=True)]
    convert_element_type x0 -> x3, local copies, waits for them, and re-layouts: none -> 19.4 us  [the longest x2 10.8 us: local(): totals.append(item.reshape(shard.shape).astype(jnp.float32))]
    reshape x2, local copies, waits for them, and re-layouts: 6.85 us -> 25.6 us  [by_width(): grad.astype(jnp.bfloat16)]
    concatenate x1, other arithmetic: 3.15 us -> 18.1 us  [local(): jnp.concatenate([by_width(item, fsdp, width) for item in grads], axis=1)]
  transfers between devices with their start and end apart: 18 -> 6, of which waited for: 14 -> 2; matrix products, arithmetic and copies ran while one was open for 8% -> 11% of each run, Pallas kernels for 1% -> 2%
where the time goes in v2:
time: 605 us; the launch traced here: 598 us
  Pallas kernels  299 us (49%)
  local copies, waits for them, and re-layouts  88.2 us (15%)
  blocking collectives  64.8 us (11%)
  matrix products  59.7 us (10%)
  other arithmetic  39.8 us (7%)
  waiting for transfers between devices  23.6 us (4%)
  between operations  14.6 us (2%)
  starting transfers between devices  8.9 us (1%)
    pallas_call x1, Pallas kernels, ring_sum(): pl.pallas_call(partial(ring_kernel, chips), out_shape=(jax.ShapeDtypeStru...  271 us
    all_to_all x2, blocking collectives, to_heads(): return lax.all_to_all(jnp.stack(parts, axis=1), 'ctx', 0, 0, tiled=True)  62.9 us
    transpose x2, local copies, waits for them, and re-layouts, by_width(): return cut.transpose(0, 2, 1, 3).reshape(fsdp, -1, width)  25.6 us
    reshape x2, local copies, waits for them, and re-layouts, by_width(): grad.astype(jnp.bfloat16)  25.6 us
    dot_general x4, matrix products, inner(): lax.dot_general(left, right, (((0,), (0,)), ((), ())), preferred_element_...  24.4 us
    concatenate x1, other arithmetic, local(): jnp.concatenate([by_width(item, fsdp, width) for item in grads], axis=1)  18.1 us
    pallas_call x1, Pallas kernels, attend_backward(): pl.pallas_call(partial(backward_kernel, head_size, min(512, length)), out...  17.3 us
    all_gather x1, waiting for transfers between devices, local(): wide_qkv = lax.all_gather(w_qkv, 'fsdp', axis=0, tiled=True)  14.4 us
  transfers between devices with their start and end apart: 6, of which 2 were waited for; matrix products, arithmetic and copies ran while one was open for 11% of the time, Pallas kernels for 2%

profile of v2, /device:TPU:0, one launch (start us, length us, event | category | flops | bytes accessed | tf_op | source)
XLA Modules:
  0.0 598.3 jit_solution(4442372895994426141)
XLA Ops:
  7.2 0.7 all-gather.5.cloned.1.call-update
  8.1 0.7 all-gather.11.cloned.1.call-update
  8.8 0.7 all-gather.7.cloned.1.call-update
  9.5 0.5 all-gather.9.cloned.1.call-update
  10.1 0.3 dynamic-update-slice.12
  10.4 0.2 dynamic-update-slice.13
  10.6 0.2 dynamic-update-slice.14
  10.8 0.2 dynamic-update-slice.15
  11.0 0.2 dynamic-update-slice.16
  11.2 0.2 dynamic-update-slice.17
  11.5 0.2 dynamic-update-slice.18
  11.7 0.2 dynamic-update-slice.19
  11.9 1.9 all_gather.15
  14.1 0.3 multiply_reduce_fusion.5
  14.4 0.3 add_convert_fusion.2
  14.7 14.4 %all-gather.5.cloned.1.call-done = bf16[1024,3072]{1,0:T(8,128)(2,1)} async-done(((bf16[512,3072]{1,0:T(8,128)(2,1)}), bf16[1024,3072]{1,0:T(8,128)(2,1)}) %all-gather.5.cloned.1.call-update) | async-done | bytes 6291472 | tf_op jit(solution)/shard_map/all_gather | solution.py:412
  29.1 4.6 fusion.33
  34.1 0.3 fusion.15
  34.7 0.2 pad_maximum_fusion.1
  34.9 44.8 %all_to_all.20.packed_ref = bf16[16,3,128,128]{3,2,1,0:T(8,128)(2,1)} all-to-all(bf16[16,3,128,128]{3,2,1,0:T(8,128)(2,1)S(1)} %pad_maximum_fusion.1), channel_id=1, replica_groups=mesh['ctx'=16,'fsdp'=2] {'ctx'}, dimensions={0} | all-to-all | bytes 3145728 | tf_op jit(solution)/shard_map/all_to_all | solution.py:170
  79.7 10.1 %attend_forward.1 = (bf16[16,128,128]{2,1,0:T(8,128)(2,1)}, f32[2,64,2048]{2,1,0:T(8,128)}, f32[2,1,2048]{2,1,0:T(1,128)}) custom-call(bf16[16,3,128,128]{3,2,1,0:T(8,128)(2,1)} %all_to_all.20.packed_ref), custom_call_target="tpu_custom_call" | custom-call | flops 1610612736 | bytes 4718592 | tf_op jit(solution)/shard_map/attend_forward/pallas_call | solution.py:127
  89.8 4.4 all-to-all-start.1
  94.3 7.8 %fusion.34 = f32[256,4096]{1,0:T(8,128)} fusion(bf16[256,1024]{1,0:T(8,128)(2,1)S(1)} %bitcast.182, bf16[4096,1024]{1,0:T(8,128)(2,1)} %all-gather.11.cloned.1.call-done), kind=kOutput, calls=%fused_computation.104 | convolution fusion | flops 2147483648 | bytes 13107200 | tf_op jit(solution)/shard_map/dot_general | solution.py:28
  102.1 6.6 %all-to-all-done.1 = bf16[16,1,128,128]{3,2,1,0:T(8,128)(2,1)S(1)} async-done(((bf16[16,1,128,128]{3,2,1,0:T(8,128)(2,1)}), bf16[16,1,128,128]{3,2,1,0:T(8,128)(2,1)S(1)}, u32[]{:S(2)}, u32[]{:S(2)}) %all-to-all-start.1) | async-done | bytes 524320 | tf_op jit(solution)/shard_map/all_to_all | solution.py:175
  108.6 0.3 copy.64
  109.0 2.6 fusion.32
  111.6 0.3 multiply_reduce_fusion.4
  111.9 11.4 %fusion.26 = (bf16[4096]{0:T(1024)(128)(2,1)S(1)}, bf16[256,4096]{1,0:T(8,128)(2,1)S(1)}, f32[256,4096]{1,0:T(8,128)}) fusion(f32[256,4096]{1,0:T(8,128)} %fusion.34, f32[4096]{0:T(1024)S(1)} %bitcast.218, bf16[1024,4096]{1,0:T(8,128)(2,1)} %all-gather.9.cloned.1.call-done, f32[256,1024]{1,0:T(8,128)S(1)} %get-tuple-element.111, f32[1024]{0:T(1024)S(1)} %bitcast.207, ...), kind=kOutput, calls=%fused_computation.98 | convolution fusion | flops 2171858944 | bytes 19957760 | tf_op jit(solution)/shard_map/dot_general | solution.py:449
  123.3 2.7 multiply_reduce_fusion
  126.0 0.4 fusion.30
  126.4 0.2 fusion.28
  126.7 0.8 copy-done.5
  127.6 0.7 fusion.10
  128.6 18.1 %all_to_all.21 = bf16[16,1,128,128]{3,2,1,0:T(8,128)(2,1)} all-to-all(bf16[16,1,128,128]{3,2,1,0:T(8,128)(2,1)S(1)} %bitcast.189), channel_id=1, replica_groups=mesh['ctx'=16,'fsdp'=2] {'ctx'}, dimensions={0} | all-to-all | bytes 1048576 | tf_op jit(solution)/shard_map/all_to_all | solution.py:170
  146.7 17.3 %attend_backward.1 = bf16[16,3,128,128]{3,2,1,0:T(8,128)(2,1)} custom-call(bf16[16,3,128,128]{3,2,1,0:T(8,128)(2,1)} %all_to_all.20.packed_ref, bf16[16,128,128]{2,1,0:T(8,128)(2,1)} %bitcast.200, f32[2,64,2048]{2,1,0:T(8,128)} %get-tuple-element.21.keep_ref, f32[2,1,2048]{2,1,0:T(1,128)} %get-tuple-element.22.lse_ref), custom_call_target="tpu_custom_call" | custom-call | flops 4294967296 | bytes 6291456 | tf_op jit(solution)/shard_map/attend_backward/pallas_call | solution.py:146
  163.9 4.4 all-to-all-start.3
  168.4 7.5 %convolution_convert_fusion.1 = bf16[1024,4096]{1,0:T(8,128)(2,1)} fusion(bf16[256,4096]{1,0:T(8,128)(2,1)} %copy-done.4, f32[256,1024]{1,0:T(8,128)S(1)} %get-tuple-element.111, f32[1024]{0:T(1024)S(1)} %bitcast.208, f32[1024]{0:T(1024)S(1)} %bitcast.206, f32[256]{0:T(256)S(1)} %fusion.22, f32[256]{0:T(256)S(1)} %broadcast_multiply_fusion), kind=kOutput, calls=%fused_computation.3 | convolution fusion | flops 2152988672 | bytes 11544576 | tf_op jit(solution)/shard_map/dot_general | solution.py:22
  175.9 14.5 %reshape.302 = bf16[2,512,4,1024]{3,2,1,0:T(4,128)(2,1)} reshape(bf16[1024,4096]{1,0:T(8,128)(2,1)} %convolution_convert_fusion.1) | data formatting | bytes 16777216 | tf_op jit(solution)/shard_map/reshape | solution.py:385
  190.4 9.6 %copy.67 = bf16[2,4,512,1024]{3,2,1,0:T(8,128)(2,1)} copy(bf16[2,4,512,1024]{3,1,2,0:T(4,128)(2,1)} %bitcast.167) | data formatting | bytes 16777216 | tf_op jit(solution)/shard_map/transpose | solution.py:386
  200.0 3.4 convolution_convert_fusion.3
  203.5 8.7 %convolution_convert_fusion = bf16[4096,1024]{1,0:T(8,128)(2,1)} fusion(bf16[256,1024]{1,0:T(8,128)(2,1)S(1)} %bitcast.183, f32[256,4096]{1,0:T(8,128)} %get-tuple-element.112), kind=kOutput, calls=%fused_computation.2 | convolution fusion | flops 2161115136 | bytes 13107200 | tf_op jit(solution)/shard_map/dot_general | solution.py:22
  212.2 3.6 fusion.9
  215.8 2.5 copy.107
  218.3 0.4 slice_reduce_fusion
  218.9 4.8 convolution_convert_fusion.2
  223.7 2.0 fusion.25
  225.7 8.6 %copy.68 = bf16[1024,3072]{0,1:T(8,128)(2,1)} copy(bf16[1024,3072]{1,0:T(8,128)(2,1)} %convolution_convert_fusion.2) | data formatting | bytes 12582912 | tf_op jit(solution)/shard_map/convert_element_type | solution.py:385
  234.3 11.1 %reshape.304 = bf16[2,512,3,1024]{1,0,3,2:T(2,128)(2,1)} reshape(bf16[1024,3072]{0,1:T(8,128)(2,1)} %copy.68) | data formatting | bytes 12582912 | tf_op jit(solution)/shard_map/reshape | solution.py:385
  245.5 16.1 %copy.69 = bf16[2,3,512,1024]{3,2,1,0:T(8,128)(2,1)} copy(bf16[2,3,512,1024]{2,0,3,1:T(2,128)(2,1)} %bitcast.170) | data formatting | bytes 12582912 | tf_op jit(solution)/shard_map/transpose | solution.py:386
  261.5 0.5 multiply_reduce_fusion.1
  262.3 0.7 pad.4
  262.9 18.1 %pad_maximum_fusion = bf16[2,6144,1024]{2,1,0:T(8,128)(2,1)} fusion(bf16[2,512,1024]{2,1,0:T(8,128)(2,1)} %bitcast.178, bf16[2,1536,1024]{2,1,0:T(8,128)(2,1)} %bitcast.169, bf16[2,2048,1024]{2,1,0:T(8,128)(2,1)} %bitcast.180, bf16[2,2048,1024]{2,1,0:T(8,128)(2,1)} %bitcast.168), kind=kLoop, calls=%fused_computation | loop fusion | flops 100663296 | bytes 50331648 | tf_op jit(solution)/shard_map/concatenate | solution.py:506
  281.0 271.3 %ring_sum.1 = (bf16[4,16,96,1024]{3,2,1,0:T(8,128)(2,1)}, bf16[16,16,128]{2,1,0:T(8,128)(2,1)}) custom-call(bf16[2,4,16,96,1024]{4,3,2,1,0:T(8,128)(2,1)} %bitcast.166, bf16[2,16,16,128]{3,2,1,0:T(8,128)(2,1)} %bitcast.198), custom_call_target="tpu_custom_call" | custom-call | tf_op jit(solution)/shard_map/ring_sum/pallas_call | solution.py:359
  552.3 2.2 slice.122
  554.5 2.8 slice_convert_fusion.1
  557.3 7.7 %slice_convert_fusion = (f32[2048,1024]{1,0:T(8,128)}, bf16[2048,1024]{1,0:T(8,128)(2,1)}) fusion(bf16[6144,1024]{1,0:T(8,128)(2,1)} %bitcast.176), kind=kLoop, calls=%fused_computation.16 | loop fusion | flops 2097152 | bytes 20971520 | tf_op jit(solution)/shard_map/convert_element_type | solution.py:512
  565.0 1.3 add_convert_fusion
  566.3 0.6 slice_bitcast_fusion
  566.9 0.6 fusion.31
  567.5 3.4 convert_bitcast_fusion.1
  570.9 6.6 %copy.70 = f32[512,3,1024]{0,2,1:T(8,128)} copy(f32[512,3,1024]{2,0,1:T(8,128)} %convert_bitcast_fusion.1) | data formatting | bytes 12582912 | tf_op jit(solution)/shard_map/convert_element_type | solution.py:512
  577.5 6.6 %copy.72 = f32[512,3072]{1,0:T(8,128)} copy(f32[512,3072]{0,1:T(8,128)} %bitcast.171) | data formatting | bytes 12582912
  584.1 3.2 convert_bitcast_fusion
  587.3 4.2 copy.73
  (114 shorter events, 2.2 us)
Async XLA Ops:
  7.2 21.9 %all-gather.5.cloned.1.call-start = ((), (), s32[]{:S(2)}) async-start(), calls=%async_computation.4 | async-start | bytes 9437184 | tf_op jit(solution)/shard_map/all_gather | solution.py:412
  7.9 2.2 copy-start.9
  7.9 2.4 copy-start.10
  7.9 2.6 copy-start.11
  7.9 2.8 copy-start.12
  8.0 3.1 copy-start.13
  8.0 3.3 copy-start.14
  8.0 3.5 copy-start.15
  8.0 3.7 copy-start.16
  8.0 3.9 copy-start.8
  8.0 5.9 copy-start
  8.0 86.3 %all-gather.11.cloned.1.call-start = ((), (), s32[]{:S(2)}) async-start(), calls=%async_computation.7 | async-start | bytes 12582912 | tf_op jit(solution)/shard_map/all_gather | solution.py:420
  8.8 100.2 %all-gather.7.cloned.1.call-start = ((), (), s32[]{:S(2)}) async-start(), calls=%async_computation.5 | async-start | bytes 3145728 | tf_op jit(solution)/shard_map/all_gather | solution.py:418
  9.5 102.4 %all-gather.9.cloned.1.call-start = ((), (), s32[]{:S(2)}) async-start(), calls=%async_computation.6 | async-start | bytes 12582912 | tf_op jit(solution)/shard_map/all_gather | solution.py:419
  14.7 19.0 %copy-start.2 = (bf16[256,1024]{1,0:T(8,128)(2,1)}, bf16[256,1024]{1,0:T(8,128)(2,1)S(1)}, u32[]{:S(2)}) copy-start(bf16[256,1024]{1,0:T(8,128)(2,1)S(1)} %add_convert_fusion.2) | copy-start | bytes 1572868
  79.7 14.6 %copy-start.1 = (bf16[2,128,1024]{2,1,0:T(8,128)(2,1)S(1)}, bf16[2,128,1024]{2,1,0:T(8,128)(2,1)}, u32[]{:S(2)}) copy-start(bf16[2,128,1024]{2,1,0:T(8,128)(2,1)} %param.16) | copy-start | bytes 1572868
  89.8 18.8 %all-to-all-start.1 = ((bf16[16,1,128,128]{3,2,1,0:T(8,128)(2,1)}), bf16[16,1,128,128]{3,2,1,0:T(8,128)(2,1)S(1)}, u32[]{:S(2)}, u32[]{:S(2)}) async-start(bf16[16,1,128,128]{3,2,1,0:T(8,128)(2,1)} %bitcast.199), calls=%async_computation.1 | async-start | bytes 1048576 | tf_op jit(solution)/shard_map/all_to_all | solution.py:175
  109.0 14.3 %copy-start.6 = (bf16[2,8,1,128,128]{4,1,3,0,2:T(8,128)(2,1)}, bf16[2,8,1,128,128]{4,1,3,0,2:T(8,128)(2,1)S(1)}, u32[]{:S(2)}) copy-start(bf16[2,8,1,128,128]{4,1,3,0,2:T(8,128)(2,1)S(1)} %copy.64) | copy-start | bytes 1572868
  111.9 11.4 %copy-start.17 = (bf16[1024,4096]{1,0:T(8,128)(2,1)S(1)}, bf16[1024,4096]{1,0:T(8,128)(2,1)}, u32[]{:S(2)}) copy-start(bf16[1024,4096]{1,0:T(8,128)(2,1)} %all-gather.9.cloned.1.call-done) | copy-start | bytes 25165828
  123.3 2.7 copy-start.4
  126.0 1.6 copy-start.18
  126.6 0.8 copy-start.5
  163.9 51.9 %all-to-all-start.3 = ((bf16[16,3,128,128]{3,2,1,0:T(8,128)(2,1)}), bf16[16,3,128,128]{3,2,1,0:T(8,128)(2,1)}, u32[]{:S(2)}, u32[]{:S(2)}) async-start(bf16[16,3,128,128]{3,2,1,0:T(8,128)(2,1)} %attend_backward.1), calls=%async_computation.3 | async-start | bytes 3145728 | tf_op jit(solution)/shard_map/all_to_all | solution.py:175
  200.0 12.2 %slice-start = ((s8[8388608]{0:T(1024)(128)(4,1)}), s8[4194304]{0:T(1024)(128)(4,1)S(1)}, s32[]{:S(2)}) async-start(s8[8388608]{0:T(1024)(128)(4,1)} %bitcast.222), calls=%async_computation.8 | async-start | bytes 8388608
  203.4 8.8 %slice-start.1 = ((s8[8388608]{0:T(1024)(128)(4,1)}), s8[4194304]{0:T(1024)(128)(4,1)S(1)}, s32[]{:S(2)}) async-start(s8[8388608]{0:T(1024)(128)(4,1)} %bitcast.222), calls=%async_computation.9 | async-start | bytes 8388608
  203.5 8.8 %copy-start.19 = (f32[256,4096]{1,0:T(8,128)S(1)}, f32[256,4096]{1,0:T(8,128)}, u32[]{:S(2)}) copy-start(f32[256,4096]{1,0:T(8,128)} %get-tuple-element.112) | copy-start | bytes 12582916
  215.8 3.1 copy-start.3
  218.7 5.0 slice-start.2
  218.9 4.8 slice-start.3
  557.3 9.0 %copy-start.7 = (bf16[16,16,128]{2,1,0:T(8,128)(2,1)S(1)}, bf16[16,16,128]{2,1,0:T(8,128)(2,1)}, u32[]{:S(2)}) copy-start(bf16[16,16,128]{2,1,0:T(8,128)(2,1)} %get-tuple-element.23) | copy-start | bytes 196612
Sparse Core Ops, SparseCore 0:
  9.6 19.5 all-gather.4
  30.7 21.0 all-gather.10
  53.3 11.7 all-gather.6
  66.4 21.0 all-gather.8

commit v3 on v2

--- a/solution.py
+++ b/solution.py
@@ -381,9 +381,12 @@
 
 
 def by_width(grad, fsdp, width):
-    rows, columns = grad.shape
-    cut = grad.astype(jnp.bfloat16).reshape(fsdp, rows // fsdp, columns // width, width)
-    return cut.transpose(0, 2, 1, 3).reshape(fsdp, -1, width)
+    rows, columns = grad.shape[0] // fsdp, grad.shape[1]
+    low = grad.astype(jnp.bfloat16)
+    return [
+        [low[half * rows : (half + 1) * rows, at : at + width] for at in range(0, columns, width)]
+        for half in range(fsdp)
+    ]
 
 
 def local(
@@ -503,13 +506,19 @@
         small = small.astype(jnp.bfloat16)
         spare = -small.shape[1] % (16 * chips)
         small = jnp.pad(small, ((0, 0), (0, spare), (0, 0))).reshape(fsdp, chips, -1, 128)
-        big = jnp.concatenate([by_width(item, fsdp, width) for item in grads], axis=1)
+        cuts = [by_width(item, fsdp, width) for item in grads]
+        big = jnp.concatenate(
+            [piece for half in range(fsdp) for cut in cuts for piece in cut[half]], axis=0
+        )
         big, rest = ring_sum(big.reshape(fsdp, 4, chips, -1, width), small)
         big, totals, at = big.reshape(-1, width), [], 0
         for shard in shards:
             count = shard.size // width
-            item = big[at : at + count].reshape(-1, shard.shape[0], width).transpose(1, 0, 2)
-            totals.append(item.reshape(shard.shape).astype(jnp.float32))
+            item = [
+                big[row : row + shard.shape[0]].astype(jnp.float32)
+                for row in range(at, at + count, shard.shape[0])
+            ]
+            totals.append(item[0] if len(item) == 1 else jnp.concatenate(item, axis=1))
             at += count
         rest = rest.reshape(-1).astype(jnp.float32)
     else:

time: 605 us -> 537 us (0.89)
  local copies, waits for them, and re-layouts: 88.2 us -> 39.8 us
  blocking collectives: 64.8 us -> 47.1 us
  other arithmetic: 39.8 us -> 23.6 us
  waiting for transfers between devices: 23.6 us -> 38.4 us
  matrix products: 59.7 us -> 53 us
    transpose x2 -> x0, local copies, waits for them, and re-layouts: 25.6 us -> none  [by_width(): return cut.transpose(0, 2, 1, 3).reshape(fsdp, -1, width)]
    reshape x2 -> x0, local copies, waits for them, and re-layouts: 25.6 us -> none  [by_width(): grad.astype(jnp.bfloat16)]
    unnamed x81 -> x111, local copies, waits for them, and re-layouts: 9.99 us -> 32.6 us
    convert_element_type x3 -> x0, local copies, waits for them, and re-layouts: 19.4 us -> none  [the longest x2 10.8 us: local(): totals.append(item.reshape(shard.shape).astype(jnp.float32))]
    all_to_all x2 -> x1, blocking collectives: 62.9 us -> 45.2 us  [to_heads(): return lax.all_to_all(jnp.stack(parts, axis=1), 'ctx', 0, 0, tiled=True)]
    concatenate x1 -> x2, other arithmetic: 18.1 us -> 7.39 us  [local(): totals.append(item[0] if len(item) == 1 else jnp.concatenate(item, axis=1))]
    all_to_all x2, waiting for transfers between devices: 6.56 us -> 16.6 us  [to_tokens(): back = lax.all_to_all(item, 'ctx', 0, 0, tiled=True)]
    dot_general x4, matrix products: 24.4 us -> 14.7 us  [inner(): lax.dot_general(left, right, (((0,), (0,)), ((), ())), preferred_element_...]
  transfers between devices with their start and end apart: 6 -> 7, of which waited for: 2 -> 4; matrix products, arithmetic and copies ran while one was open for 11% -> 8% of each run, Pallas kernels for 2% -> 2%
where the time goes in v3:
time: 537 us; the launch traced here: 532 us
  Pallas kernels  302 us (56%)
  matrix products  53 us (10%)
  blocking collectives  47.1 us (9%)
  local copies, waits for them, and re-layouts  39.8 us (7%)
  waiting for transfers between devices  38.4 us (7%)
  other arithmetic  23.6 us (4%)
  between operations  14.7 us (3%)
  starting transfers between devices  13.5 us (3%)
    pallas_call x1, Pallas kernels, ring_sum(): pl.pallas_call(partial(ring_kernel, chips), out_shape=(jax.ShapeDtypeStru...  274 us
    all_to_all x1, blocking collectives, to_heads(): return lax.all_to_all(jnp.stack(parts, axis=1), 'ctx', 0, 0, tiled=True)  45.2 us
    unnamed x111, local copies, waits for them, and re-layouts  32.6 us
    pallas_call x1, Pallas kernels, attend_backward(): pl.pallas_call(partial(backward_kernel, head_size, min(512, length)), out...  17.3 us
    all_to_all x2, waiting for transfers between devices, to_tokens(): back = lax.all_to_all(item, 'ctx', 0, 0, tiled=True)  16.6 us
    dot_general x4, matrix products, times_transposed(): lax.dot_general(left, right, (((1,), (1,)), ((), ())), preferred_element_...  16.1 us
    dot_general x4, matrix products, inner(): lax.dot_general(left, right, (((0,), (0,)), ((), ())), preferred_element_...  14.7 us
    all_gather x1, waiting for transfers between devices, local(): wide_qkv = lax.all_gather(w_qkv, 'fsdp', axis=0, tiled=True)  14.4 us
  transfers between devices with their start and end apart: 7, of which 4 were waited for; matrix products, arithmetic and copies ran while one was open for 8% of the time, Pallas kernels for 2%

profile of v3, /device:TPU:0, one launch (start us, length us, event | category | flops | bytes accessed | tf_op | source)
XLA Modules:
  0.0 531.9 jit_solution(485553766489410765)
XLA Ops:
  7.2 0.7 all-gather.5.cloned.1.call-update
  8.1 0.7 all-gather.11.cloned.1.call-update
  8.8 0.7 all-gather.7.cloned.1.call-update
  9.5 0.5 all-gather.9.cloned.1.call-update
  11.9 1.9 all_gather.15
  14.4 0.3 add_convert_fusion.2
  14.7 14.4 %all-gather.5.cloned.1.call-done = bf16[1024,3072]{1,0:T(8,128)(2,1)} async-done(((bf16[512,3072]{1,0:T(8,128)(2,1)}), bf16[1024,3072]{1,0:T(8,128)(2,1)}) %all-gather.5.cloned.1.call-update) | async-done | bytes 6291472 | tf_op jit(solution)/shard_map/all_gather | solution.py:415
  29.1 4.6 fusion.34
  34.9 45.2 %all_to_all.20.packed_ref = bf16[16,3,128,128]{3,2,1,0:T(8,128)(2,1)} all-to-all(bf16[16,3,128,128]{3,2,1,0:T(8,128)(2,1)S(1)} %pad_maximum_fusion), channel_id=1, replica_groups=mesh['ctx'=16,'fsdp'=2] {'ctx'}, dimensions={0} | all-to-all | bytes 3145728 | tf_op jit(solution)/shard_map/all_to_all | solution.py:170
  80.1 10.1 %attend_forward.1 = (bf16[16,128,128]{2,1,0:T(8,128)(2,1)}, f32[2,64,2048]{2,1,0:T(8,128)}, f32[2,1,2048]{2,1,0:T(1,128)}) custom-call(bf16[16,3,128,128]{3,2,1,0:T(8,128)(2,1)} %all_to_all.20.packed_ref), custom_call_target="tpu_custom_call" | custom-call | flops 1610612736 | bytes 4718592 | tf_op jit(solution)/shard_map/attend_forward/pallas_call | solution.py:127
  90.2 4.3 all-to-all-start.1
  94.7 7.8 %fusion.35 = f32[256,4096]{1,0:T(8,128)} fusion(bf16[256,1024]{1,0:T(8,128)(2,1)S(1)} %bitcast.156, bf16[4096,1024]{1,0:T(8,128)(2,1)} %all-gather.11.cloned.1.call-done), kind=kOutput, calls=%fused_computation.122 | convolution fusion | flops 2147483648 | bytes 13107200 | tf_op jit(solution)/shard_map/dot_general | solution.py:28
  102.5 6.4 %all-to-all-done.1 = bf16[16,1,128,128]{3,2,1,0:T(8,128)(2,1)S(1)} async-done(((bf16[16,1,128,128]{3,2,1,0:T(8,128)(2,1)}), bf16[16,1,128,128]{3,2,1,0:T(8,128)(2,1)S(1)}, u32[]{:S(2)}, u32[]{:S(2)}) %all-to-all-start.1) | async-done | bytes 524320 | tf_op jit(solution)/shard_map/all_to_all | solution.py:175
  108.9 0.3 copy.44
  109.3 2.6 fusion.33
  112.2 11.4 %fusion.26 = (bf16[4096]{0:T(1024)(128)(2,1)S(1)}, bf16[256,4096]{1,0:T(8,128)(2,1)S(1)}, f32[256,4096]{1,0:T(8,128)}) fusion(f32[256,4096]{1,0:T(8,128)} %fusion.35, f32[4096]{0:T(1024)S(1)} %bitcast.191, bf16[1024,4096]{1,0:T(8,128)(2,1)} %all-gather.9.cloned.1.call-done, f32[256,1024]{1,0:T(8,128)S(1)} %get-tuple-element.72, f32[1024]{0:T(1024)S(1)} %bitcast.180, ...), kind=kOutput, calls=%fused_computation.115 | convolution fusion | flops 2171858944 | bytes 19957760 | tf_op jit(solution)/shard_map/dot_general | solution.py:452
  123.7 2.7 multiply_reduce_fusion
  126.4 0.4 fusion.30
  127.0 0.8 copy-done.10
  127.9 0.7 fusion.10
  128.8 0.9 copy.45
  129.7 4.6 all-to-all-start.2
  134.4 4.1 convolution_convert_fusion.1
  138.5 1.2 slice_dynamic-update-slice_fusion.17
  139.6 2.5 copy-done
  142.2 1.1 slice_dynamic-update-slice_fusion.16
  143.3 4.7 all-to-all-done.2
  148.0 17.3 %attend_backward.1 = bf16[16,3,128,128]{3,2,1,0:T(8,128)(2,1)} custom-call(bf16[16,3,128,128]{3,2,1,0:T(8,128)(2,1)} %all_to_all.20.packed_ref, bf16[16,128,128]{2,1,0:T(8,128)(2,1)} %bitcast.18.grad_ref, f32[2,64,2048]{2,1,0:T(8,128)} %get-tuple-element.21.keep_ref, f32[2,1,2048]{2,1,0:T(1,128)} %get-tuple-element.22.lse_ref), custom_call_target="tpu_custom_call" | custom-call | flops 4294967296 | bytes 6291456 | tf_op jit(solution)/shard_map/attend_backward/pallas_call | solution.py:146
  165.3 4.4 all-to-all-start.3
  169.7 2.3 slice_dynamic-update-slice_fusion.15
  172.0 2.3 slice_dynamic-update-slice_fusion.14
  174.3 3.4 convolution_convert_fusion.3
  177.7 5.3 %convolution_convert_fusion = bf16[4096,1024]{1,0:T(8,128)(2,1)S(1)} fusion(bf16[256,1024]{1,0:T(8,128)(2,1)S(1)} %bitcast.157, f32[256,4096]{1,0:T(8,128)} %get-tuple-element.73), kind=kOutput, calls=%fused_computation | convolution fusion | flops 2161115136 | bytes 13107200 | tf_op jit(solution)/shard_map/dot_general | solution.py:22
  183.0 2.5 slice_dynamic-update-slice_fusion.1
  185.5 3.1 copy-done.3
  188.6 3.7 fusion.9
  192.3 10.2 %all-to-all-done.3 = bf16[16,3,128,128]{3,2,1,0:T(8,128)(2,1)} async-done(((bf16[16,3,128,128]{3,2,1,0:T(8,128)(2,1)}), bf16[16,3,128,128]{3,2,1,0:T(8,128)(2,1)}, u32[]{:S(2)}, u32[]{:S(2)}) %all-to-all-start.3) | async-done | bytes 1572896 | tf_op jit(solution)/shard_map/all_to_all | solution.py:175
  202.4 2.5 copy.80
  204.9 0.4 slice_reduce_fusion
  205.6 1.9 convolution_convert_fusion.2
  207.5 4.9 fusion.25
  212.4 1.1 slice_dynamic-update-slice_fusion.13
  213.5 1.1 slice_dynamic-update-slice_fusion.12
  214.6 1.0 slice_dynamic-update-slice_fusion.11
  215.6 1.1 slice_dynamic-update-slice_fusion.10
  216.7 1.1 slice_dynamic-update-slice_fusion.9
  217.8 1.2 slice_dynamic-update-slice_fusion.8
  219.0 1.1 slice_dynamic-update-slice_fusion.7
  220.1 1.0 slice_dynamic-update-slice_fusion.6
  221.1 2.4 slice_dynamic-update-slice_fusion
  223.5 1.0 slice_dynamic-update-slice_fusion.5
  224.6 1.1 slice_dynamic-update-slice_fusion.4
  225.6 1.1 slice_dynamic-update-slice_fusion.3
  226.7 1.1 slice_dynamic-update-slice_fusion.2
  227.8 0.6 multiply_reduce_fusion.1
  228.6 0.7 pad.4
  229.2 274.3 %ring_sum.1 = (bf16[4,16,96,1024]{3,2,1,0:T(8,128)(2,1)}, bf16[16,16,128]{2,1,0:T(8,128)(2,1)}) custom-call(bf16[2,4,16,96,1024]{4,3,2,1,0:T(8,128)(2,1)} %bitcast.149, bf16[2,16,16,128]{3,2,1,0:T(8,128)(2,1)} %bitcast.172), custom_call_target="tpu_custom_call" | custom-call | tf_op jit(solution)/shard_map/ring_sum/pallas_call | solution.py:359
  503.6 4.9 fusion.31
  508.5 6.7 %slice_convert_fusion = f32[2048,1024]{1,0:T(8,128)} fusion(bf16[6144,1024]{1,0:T(8,128)(2,1)} %bitcast.152), kind=kLoop, calls=%fused_computation.13 | loop fusion | flops 2097152 | bytes 12582912 | tf_op jit(solution)/shard_map/convert_element_type | solution.py:518
  515.2 1.3 add_convert_fusion
  516.6 0.6 slice_bitcast_fusion
  517.2 0.6 fusion.32
  517.8 3.5 maximum_convert_fusion.1
  521.3 3.9 maximum_convert_fusion
  (138 shorter events, 5.1 us)
Async XLA Ops:
  7.2 21.9 %all-gather.5.cloned.1.call-start = ((), (), s32[]{:S(2)}) async-start(), calls=%async_computation.4 | async-start | bytes 9437184 | tf_op jit(solution)/shard_map/all_gather | solution.py:415
  7.9 2.2 copy-start.14
  7.9 2.4 copy-start.15
  7.9 2.6 copy-start.16
  7.9 2.8 copy-start.17
  8.0 3.1 copy-start.18
  8.0 3.3 copy-start.19
  8.0 3.5 copy-start.20
  8.0 3.7 copy-start.21
  8.0 3.9 copy-start.13
  8.0 5.9 %copy-start.1 = (bf16[2,128,1024]{2,1,0:T(8,128)(2,1)S(1)}, bf16[2,128,1024]{2,1,0:T(8,128)(2,1)}, u32[]{:S(2)}) copy-start(bf16[2,128,1024]{2,1,0:T(8,128)(2,1)} %param.15) | copy-start | bytes 1572868
  8.0 86.7 %all-gather.11.cloned.1.call-start = ((), (), s32[]{:S(2)}) async-start(), calls=%async_computation.7 | async-start | bytes 12582912 | tf_op jit(solution)/shard_map/all_gather | solution.py:423
  8.8 100.6 %all-gather.7.cloned.1.call-start = ((), (), s32[]{:S(2)}) async-start(), calls=%async_computation.5 | async-start | bytes 3145728 | tf_op jit(solution)/shard_map/all_gather | solution.py:421
  9.5 102.7 %all-gather.9.cloned.1.call-start = ((), (), s32[]{:S(2)}) async-start(), calls=%async_computation.6 | async-start | bytes 12582912 | tf_op jit(solution)/shard_map/all_gather | solution.py:422
  14.7 19.0 %copy-start.7 = (bf16[256,1024]{1,0:T(8,128)(2,1)}, bf16[256,1024]{1,0:T(8,128)(2,1)S(1)}, u32[]{:S(2)}) copy-start(bf16[256,1024]{1,0:T(8,128)(2,1)S(1)} %add_convert_fusion.2) | copy-start | bytes 1572868
  80.1 14.5 %copy-start.4 = (bf16[2,128,1024]{2,1,0:T(8,128)(2,1)S(1)}, bf16[2,128,1024]{2,1,0:T(8,128)(2,1)}, u32[]{:S(2)}) copy-start(bf16[2,128,1024]{2,1,0:T(8,128)(2,1)} %param.16) | copy-start | bytes 1572868
  90.2 18.8 %all-to-all-start.1 = ((bf16[16,1,128,128]{3,2,1,0:T(8,128)(2,1)}), bf16[16,1,128,128]{3,2,1,0:T(8,128)(2,1)S(1)}, u32[]{:S(2)}, u32[]{:S(2)}) async-start(bf16[16,1,128,128]{3,2,1,0:T(8,128)(2,1)} %bitcast.173), calls=%async_computation.1 | async-start | bytes 1048576 | tf_op jit(solution)/shard_map/all_to_all | solution.py:175
  109.3 14.4 %copy-start.11 = (bf16[2,8,1,128,128]{4,1,3,0,2:T(8,128)(2,1)}, bf16[2,8,1,128,128]{4,1,3,0,2:T(8,128)(2,1)S(1)}, u32[]{:S(2)}) copy-start(bf16[2,8,1,128,128]{4,1,3,0,2:T(8,128)(2,1)S(1)} %copy.44) | copy-start | bytes 1572868
  112.2 11.4 %copy-start.22 = (bf16[1024,4096]{1,0:T(8,128)(2,1)S(1)}, bf16[1024,4096]{1,0:T(8,128)(2,1)}, u32[]{:S(2)}) copy-start(bf16[1024,4096]{1,0:T(8,128)(2,1)} %all-gather.9.cloned.1.call-done) | copy-start | bytes 25165828
  123.6 2.7 copy-start.9
  126.3 1.6 copy-start.23
  127.0 0.8 copy-start.10
  129.7 18.3 %all-to-all-start.2 = ((bf16[16,1,128,128]{3,2,1,0:T(8,128)(2,1)}), bf16[16,1,128,128]{3,2,1,0:T(8,128)(2,1)}, u32[]{:S(2)}, u32[]{:S(2)}) async-start(bf16[16,1,128,128]{3,2,1,0:T(8,128)(2,1)} %bitcast.159), calls=%async_computation.2 | async-start | bytes 1048576 | tf_op jit(solution)/shard_map/all_to_all | solution.py:170
  138.5 3.7 copy-start
  165.3 37.2 %all-to-all-start.3 = ((bf16[16,3,128,128]{3,2,1,0:T(8,128)(2,1)}), bf16[16,3,128,128]{3,2,1,0:T(8,128)(2,1)}, u32[]{:S(2)}, u32[]{:S(2)}) async-start(bf16[16,3,128,128]{3,2,1,0:T(8,128)(2,1)} %attend_backward.1), calls=%async_computation.3 | async-start | bytes 3145728 | tf_op jit(solution)/shard_map/all_to_all | solution.py:175
  174.3 14.4 %slice-start.4 = ((s8[8388608]{0:T(1024)(128)(4,1)}), s8[4194304]{0:T(1024)(128)(4,1)S(1)}, s32[]{:S(2)}) async-start(s8[8388608]{0:T(1024)(128)(4,1)} %bitcast.195), calls=%async_computation.12 | async-start | bytes 8388608
  177.7 10.9 %slice-start.5 = ((s8[8388608]{0:T(1024)(128)(4,1)}), s8[4194304]{0:T(1024)(128)(4,1)S(1)}, s32[]{:S(2)}) async-start(s8[8388608]{0:T(1024)(128)(4,1)} %bitcast.195), calls=%async_computation.13 | async-start | bytes 8388608
  183.0 5.6 %copy-start.3 = (bf16[4096,1024]{1,0:T(8,128)(2,1)}, bf16[4096,1024]{1,0:T(8,128)(2,1)S(1)}, u32[]{:S(2)}) copy-start(bf16[4096,1024]{1,0:T(8,128)(2,1)S(1)} %convolution_convert_fusion) | copy-start | bytes 25165828
  183.0 5.6 %copy-start.24 = (f32[256,4096]{1,0:T(8,128)S(1)}, f32[256,4096]{1,0:T(8,128)}, u32[]{:S(2)}) copy-start(f32[256,4096]{1,0:T(8,128)} %get-tuple-element.73) | copy-start | bytes 12582916
  202.4 3.1 copy-start.8
  205.6 11.1 %slice-start = ((s8[8388608]{0:T(1024)(128)(4,1)}), s8[4194304]{0:T(1024)(128)(4,1)S(1)}, s32[]{:S(2)}) async-start(s8[8388608]{0:T(1024)(128)(4,1)} %bitcast.147), calls=%async_computation.8 | async-start | bytes 8388608
  207.4 9.3 %slice-start.1 = ((s8[8388608]{0:T(1024)(128)(4,1)}), s8[4194304]{0:T(1024)(128)(4,1)S(1)}, s32[]{:S(2)}) async-start(s8[8388608]{0:T(1024)(128)(4,1)} %bitcast.147), calls=%async_computation.9 | async-start | bytes 8388608
  207.4 13.7 %slice-start.2 = ((s8[8388608]{0:T(1024)(128)(4,1)}), s8[4194304]{0:T(1024)(128)(4,1)S(1)}, s32[]{:S(2)}) async-start(s8[8388608]{0:T(1024)(128)(4,1)} %bitcast.153), calls=%async_computation.10 | async-start | bytes 8388608
  212.4 15.4 %copy-start.5 = (f32[256,1024]{1,0:T(8,128)}, f32[256,1024]{1,0:T(8,128)S(1)}, u32[]{:S(2)}) copy-start(f32[256,1024]{1,0:T(8,128)S(1)} %get-tuple-element.75) | copy-start | bytes 3145732
  212.4 3.3 copy-start.2
  213.5 7.6 %slice-start.3 = ((s8[8388608]{0:T(1024)(128)(4,1)}), s8[4194304]{0:T(1024)(128)(4,1)S(1)}, s32[]{:S(2)}) async-start(s8[8388608]{0:T(1024)(128)(4,1)} %bitcast.153), calls=%async_computation.11 | async-start | bytes 8388608
  508.5 6.7 %copy-start.6 = (f32[256,1024]{1,0:T(8,128)S(1)}, f32[256,1024]{1,0:T(8,128)}, u32[]{:S(2)}) copy-start(f32[256,1024]{1,0:T(8,128)} %copy-done.5) | copy-start | bytes 3145732
  508.5 8.0 %copy-start.12 = (bf16[16,16,128]{2,1,0:T(8,128)(2,1)S(1)}, bf16[16,16,128]{2,1,0:T(8,128)(2,1)}, u32[]{:S(2)}) copy-start(bf16[16,16,128]{2,1,0:T(8,128)(2,1)} %get-tuple-element.23) | copy-start | bytes 196612
Sparse Core Ops, SparseCore 0:
  9.6 19.5 all-gather.4
  30.7 21.0 all-gather.10
  53.3 11.7 all-gather.6
  66.4 21.0 all-gather.8
